TPU v7x, 32 devices: a whole 2x2x4 slice. The times are simulated.
32 devices in a mesh: gx: 4 (over z), gy: 4 (over x, core), gz: 2 (over y).
Axes of the slice: x: 2, y: 2, z: 4, core: 2. Of those that a mesh axis runs over, the one named last changes fastest.
Arguments:
- orbitals: float32 [4, 4, 2, 96, 4096], P('gx', 'gy', 'gz'), may hold values from -6 to 6
- potential: float32 [32, 32, 16], P('gx', 'gy', 'gz'), may hold values from -1.5 to 1.5
- coefficients: float32 [4, 4, 2, 96, 256], P('gx', 'gy', 'gz'), may hold values from -0.6 to 0.6
Outputs:
- filtered_coefficients: float32 [4, 4, 2, 96, 256], P('gx', 'gy', 'gz')
All inputs are finite; a program needn't handle non-finite values.
Results may differ from a plain program's by a relative error of at most 0.0003.
Values sent between devices are 32-bit elements; how exact they have to be, the bound alone decides.
A program may use at most 64 MiB of HBM per device.

v0:
```python
import jax
import jax.numpy as jnp
from jax import lax
from jax.sharding import PartitionSpec as P

CHEB = 2
NEWTON = 6
DG_STEPS = 3


cutoff = 1.0


def passed_along(shard, axis, by):
    devices = lax.axis_size(axis)
    return lax.ppermute(shard, axis, [(i, (i + by) % devices) for i in range(devices)])


def extended(cells, sides, width):
    for axis, dim in sides:
        count = lax.axis_size(axis)
        head = lax.slice_in_dim(cells, 0, width, axis=dim)
        tail = lax.slice_in_dim(cells, cells.shape[dim] - width, cells.shape[dim], axis=dim)
        cells = jnp.concatenate(
            [
                lax.ppermute(tail, axis, [(i, (i + 1) % count) for i in range(count)]),
                cells,
                lax.ppermute(head, axis, [((i + 1) % count, i) for i in range(count)]),
            ],
            axis=dim,
        )
    return cells


def matmul(left, right):
    return jnp.dot(left, right, precision=lax.Precision.HIGHEST, preferred_element_type=jnp.float32)


def box_masks(length):
    position = jnp.arange(length**3, dtype=jnp.int32)
    coordinates = (position // (length * length), position // length % length, position % length)
    mask_list = []
    for coordinate, stride in zip(coordinates, (length * length, length, 1)):
        mask_list.append(
            (
                stride,
                (coordinate > 0).astype(jnp.float32),
                (coordinate < length - 1).astype(jnp.float32),
            )
        )
    return mask_list


def apply_box(vectors, potential_flat, length):
    area = length * length
    cells = length**3
    padded = jnp.pad(vectors, ((0, 0), (area, area)))
    total = jnp.zeros_like(vectors)
    for stride, lower_ok, upper_ok in box_masks(length):
        total = (
            total
            + lower_ok * padded[:, area - stride : area - stride + cells]
            + upper_ok * padded[:, area + stride : area + stride + cells]
        )
    return (3.0 + potential_flat) * vectors - 0.5 * total


def chebyshev(operator, initial, degree, centre, half_width):
    prior_vectors = initial
    current = (operator(initial) - centre * initial) / half_width
    for repeat in range(degree - 1):
        following = 2.0 * (operator(current) - centre * current) / half_width - prior_vectors
        prior_vectors, current = (current, following)
    return current


def inverse_root(intersection, newton_count):
    sigma = jnp.sqrt(jnp.sum(intersection * intersection))
    identity = jnp.eye(intersection.shape[0], dtype=jnp.float32)
    current = intersection / sigma
    inverse = identity
    for repeat in range(newton_count):
        factor = 1.5 * identity - 0.5 * matmul(inverse, current)
        current = matmul(current, factor)
        inverse = matmul(factor, inverse)
    return inverse / jnp.sqrt(sigma)


def element_basis(orbital_rows, ext_potential, length, centre, half_width):
    doubled = 2 * length
    potential_flat = ext_potential.reshape(doubled**3)

    def extended_operator(vectors):
        return apply_box(vectors, potential_flat, doubled)

    filtered = chebyshev(extended_operator, orbital_rows, CHEB, centre, half_width)
    lower = length // 2
    restricted = filtered.reshape(-1, doubled, doubled, doubled)[
        :, lower : lower + length, lower : lower + length, lower : lower + length
    ]
    restricted = restricted.reshape(-1, length**3)
    intersection = matmul(restricted, restricted.T)
    basis = matmul(inverse_root(intersection, NEWTON), restricted)
    own_potential = ext_potential[
        lower : lower + length, lower : lower + length, lower : lower + length
    ].reshape(length**3)
    diagonal_block = matmul(basis, apply_box(basis, own_potential, length).T)
    return (basis, diagonal_block)


def face_layers(basis, length):
    cube = basis.reshape(-1, length, length, length)
    flat = length * length
    return (
        cube[:, 0, :, :].reshape(-1, flat),
        cube[:, length - 1, :, :].reshape(-1, flat),
        cube[:, :, 0, :].reshape(-1, flat),
        cube[:, :, length - 1, :].reshape(-1, flat),
        cube[:, :, :, 0].reshape(-1, flat),
        cube[:, :, :, length - 1].reshape(-1, flat),
    )


def per_device(orbitals, potential, coefficients):
    length = potential.shape[0]
    spectrum_top = 6.0 + lax.pmax(jnp.max(potential), ("gx", "gy", "gz"))
    centre = (spectrum_top + cutoff) / 2.0
    half_width = (spectrum_top - cutoff) / 2.0
    along_x = jnp.concatenate([passed_along(potential, "gx", 1), potential], axis=0)
    along_y = jnp.concatenate([passed_along(along_x, "gy", 1), along_x], axis=1)
    ext_potential = jnp.concatenate([passed_along(along_y, "gz", 1), along_y], axis=2)
    basis, diagonal_block = element_basis(
        orbitals[0, 0, 0], ext_potential, length, centre, half_width
    )
    faces = face_layers(basis, length)

    def galerkin(vectors):
        projected = [matmul(own_face.T, vectors) for own_face in faces]
        got_x = extended(jnp.stack([projected[0], projected[1]]), (("gx", 0),), 1)
        got_y = extended(jnp.stack([projected[2], projected[3]]), (("gy", 0),), 1)
        got_z = extended(jnp.stack([projected[4], projected[5]]), (("gz", 0),), 1)
        result = matmul(diagonal_block, vectors)
        incoming = (got_x[0], got_x[3], got_y[0], got_y[3], got_z[0], got_z[3])
        for own_face, carried in zip(faces, incoming):
            result = result + -0.5 * matmul(own_face, carried)
        return result

    filtered = chebyshev(galerkin, coefficients[0, 0, 0], DG_STEPS, centre, half_width)
    return filtered.reshape(coefficients.shape)


def solution(mesh):
    placed = (P("gx", "gy", "gz", None, None), P("gx", "gy", "gz"), P("gx", "gy", "gz", None, None))
    return jax.shard_map(
        per_device,
        mesh=mesh,
        in_specs=placed,
        out_specs=P("gx", "gy", "gz", None, None),
        check_vma=False,
    )
```

profile of v0, /device:TPU:0, one launch (start us, length us, event | category | flops | bytes accessed | tf_op | source)
XLA Modules:
  0.0 113.2 jit_solution(2863147310436125498)
XLA Ops:
  0.0 3.0 %collective-permute-start = (f32[8,8,8]{2,1,0:T(8,128)}, f32[8,8,8]{2,1,0:T(8,128)S(1)}, u32[]{:S(2)}, u32[]{:S(2)}) collective-permute-start(f32[8,8,8]{2,1,0:T(8,128)} %param.4), channel_id=1, source_target_pairs={{0,8},{8,16},{16,24},{24,0},{1,9},{9,17},{17,25},{25,1},{2,10},{10... | collective-permute-start | bytes 6152 | tf_op jit(solution)/shard_map/ppermute | solution.py:16
  3.1 4.1 %collective-permute-done = f32[8,8,8]{2,1,0:T(8,128)S(1)} collective-permute-done((f32[8,8,8]{2,1,0:T(8,128)}, f32[8,8,8]{2,1,0:T(8,128)S(1)}, u32[]{:S(2)}, u32[]{:S(2)}) %collective-permute-start) | collective-permute-done | bytes 2080 | tf_op jit(solution)/shard_map/ppermute | solution.py:16
  7.2 1.4 %constant_dynamic-update-slice_fusion = (f32[16,8,8]{2,1,0:T(8,128)S(1)}, f32[]{:T(128)}) fusion(f32[16,8,8]{2,1,0:T(8,128)S(1)} %constant_dynamic-update-slice_fusion.1, f32[8,8,8]{2,1,0:T(8,128)} %param.4), kind=kLoop, calls=%fused_computation.221 | loop fusion | flops 511 | bytes 34820 | tf_op jit(solution)/shard_map/concatenate | solution.py:129
  8.5 3.7 %collective-permute-done.1 = f32[16,8,8]{2,1,0:T(8,128)S(1)} collective-permute-done((f32[16,8,8]{2,1,0:T(8,128)S(1)}, f32[16,8,8]{2,1,0:T(8,128)S(1)}, u32[]{:S(2)}, u32[]{:S(2)}) %collective-permute-start.1) | collective-permute-done | bytes 4128 | tf_op jit(solution)/shard_map/ppermute | solution.py:16
  12.2 1.8 %collective-permute-start.2 = (f32[16,16,8]{2,1,0:T(8,128)S(1)}, f32[16,16,8]{2,1,0:T(8,128)S(1)}, u32[]{:S(2)}, u32[]{:S(2)}) collective-permute-start(f32[16,16,8]{2,1,0:T(8,128)S(1)} %pad_maximum_fusion), channel_id=1, source_target_pairs={{0,1},{1,0},{2,3},{3,2},{4,5},{5,4},{6,7},{7,6},{8,9},{9,8},{10,11... | collective-permute-start | bytes 24584 | tf_op jit(solution)/shard_map/ppermute | solution.py:16
  14.0 38.0 %pmax.7 = f32[]{:T(128)} all-reduce(f32[]{:T(128)} %get-tuple-element.10), channel_id=1, replica_groups=mesh['gx'=4,'gy'=4,'gz'=2] {'gx','gy','gz'}, use_global_device_ids=true, to_apply=%region_1.0 | all-reduce | flops 1 | bytes 8 | tf_op jit(solution)/shard_map/pmax | solution.py:126
  53.5 7.5 %fusion.9 = f32[96,4096]{1,0:T(8,128)S(1)} fusion(f32[96,4096]{1,0:T(8,128)} %bitcast.216, f32[]{:T(128)S(6)} %div.95, f32[]{:T(128)S(6)} %div.94, f32[4096]{0:T(1024)S(1)} %get-tuple-element.16, f32[4096]{0:T(1024)S(1)} %get-tuple-element.15, f32[4096]{0:T(1024)S(1)} %get-tuple-element.17, f32[4096]{0:T(1024)S(1)} %get-tuple-element.18, ...), kind=kLoop, calls=%fused_computation.21 | loop fusion | flops 6684672 | bytes 3260424 | tf_op jit(solution)/shard_map/div | solution.py:70
  61.1 1.7 %fusion.26 = f32[96,4096]{1,0:T(8,128)S(1)} fusion(f32[96,4096]{1,0:T(8,128)S(1)} %fusion.9, f32[]{:T(128)S(6)} %div.95, f32[]{:T(128)S(6)} %div.94, f32[4096]{0:T(1024)S(1)} %get-tuple-element.16, f32[4096]{0:T(1024)S(1)} %get-tuple-element.15, f32[4096]{0:T(1024)S(1)} %get-tuple-element.17, f32[4096]{0:T(1024)S(1)} %get-tuple-element.18, ...), kind=kLoop, calls=%fused_computation.38 | loop fusion | flops 7471104 | bytes 4833288 | tf_op jit(solution)/shard_map/sub | solution.py:72
  62.8 1.8 %copy.5 = f32[96,4096]{0,1:T(8,128)} copy(f32[96,4096]{1,0:T(8,128)S(1)} %fusion.26) | data formatting | bytes 3145728 | tf_op jit(solution)/shard_map/sub | solution.py:72
  64.6 2.4 %multiply_reduce_fusion = (f32[]{:T(128)}, f32[96,96]{1,0:T(8,128)S(1)}) fusion(f32[96,16,16,16]{0,3,2,1:T(8,128)} %bitcast.242), kind=kOutput, calls=%fused_computation.182 | convolution fusion | flops 56641536 | bytes 299012 | tf_op jit(solution)/shard_map/dot_general | solution.py:36
  67.0 1.1 slice.104
  72.0 0.4 fusion.167
  73.8 2.5 %collective-permute-start.8 = (f32[1,64,256]{2,1,0:T(8,128)S(1)}, f32[1,64,256]{2,1,0:T(8,128)S(1)}, u32[]{:S(2)}, u32[]{:S(2)}) collective-permute-start(f32[1,64,256]{2,1,0:T(8,128)S(1)} %convolution_bitcast_fusion.12), channel_id=1, source_target_pairs={{1,0},{0,1},{3,2},{2,3},{5,4},{4,5},{7,6},{6,7},{9,8},{8,9},{11,10... | collective-permute-start | bytes 196616 | tf_op jit(solution)/shard_map/ppermute | solution.py:28
  76.4 2.0 %collective-permute-start.3 = (f32[1,64,256]{2,1,0:T(8,128)S(1)}, f32[1,64,256]{2,1,0:T(8,128)S(1)}, u32[]{:S(2)}, u32[]{:S(2)}) collective-permute-start(f32[1,64,256]{2,1,0:T(8,128)S(1)} %convolution_bitcast_fusion.17), channel_id=1, source_target_pairs={{0,8},{8,16},{16,24},{24,0},{1,9},{9,17},{17,25},{25,1},{2,10},{10... | collective-permute-start | bytes 196616 | tf_op jit(solution)/shard_map/ppermute | solution.py:26
  78.4 1.9 %collective-permute-start.4 = (f32[1,64,256]{2,1,0:T(8,128)S(1)}, f32[1,64,256]{2,1,0:T(8,128)S(1)}, u32[]{:S(2)}, u32[]{:S(2)}) collective-permute-start(f32[1,64,256]{2,1,0:T(8,128)S(1)} %convolution_bitcast_fusion.16), channel_id=1, source_target_pairs={{8,0},{16,8},{24,16},{0,24},{9,1},{17,9},{25,17},{1,25},{10,2},{18... | collective-permute-start | bytes 196616 | tf_op jit(solution)/shard_map/ppermute | solution.py:28
  80.2 0.7 fusion.75
  81.3 1.2 %collective-permute-done.3 = f32[1,64,256]{2,1,0:T(8,128)S(1)} collective-permute-done((f32[1,64,256]{2,1,0:T(8,128)S(1)}, f32[1,64,256]{2,1,0:T(8,128)S(1)}, u32[]{:S(2)}, u32[]{:S(2)}) %collective-permute-start.3) | collective-permute-done | bytes 65568 | tf_op jit(solution)/shard_map/ppermute | solution.py:26
  82.5 0.3 collective-permute-start.6
  82.8 0.3 fusion.40
  83.1 0.4 collective-permute-done.4
  83.5 0.3 fusion.39
  83.8 0.3 convolution_multiply_fusion.12
  84.1 0.3 convolution_multiply_fusion.13
  84.4 0.4 collective-permute-done.6
  85.0 0.3 fusion.60
  86.9 3.6 %collective-permute-start.10 = (f32[1,64,256]{2,1,0:T(8,128)S(1)}, f32[1,64,256]{2,1,0:T(8,128)S(1)}, u32[]{:S(2)}, u32[]{:S(2)}) collective-permute-start(f32[1,64,256]{2,1,0:T(8,128)S(1)} %convolution_bitcast_fusion.10), channel_id=1, source_target_pairs={{8,0},{16,8},{24,16},{0,24},{9,1},{17,9},{25,17},{1,25},{10,2},{18... | collective-permute-start | bytes 196616 | tf_op jit(solution)/shard_map/ppermute | solution.py:28
  90.5 1.6 %collective-permute-start.11 = (f32[1,64,256]{2,1,0:T(8,128)S(1)}, f32[1,64,256]{2,1,0:T(8,128)S(1)}, u32[]{:S(2)}, u32[]{:S(2)}) collective-permute-start(f32[1,64,256]{2,1,0:T(8,128)S(1)} %convolution_bitcast_fusion.9), channel_id=1, source_target_pairs={{0,2},{2,4},{4,6},{6,0},{1,3},{3,5},{5,7},{7,1},{8,10},{10,12},{12... | collective-permute-start | bytes 196616 | tf_op jit(solution)/shard_map/ppermute | solution.py:26
  92.3 1.9 %collective-permute-start.13 = (f32[1,64,256]{2,1,0:T(8,128)S(1)}, f32[1,64,256]{2,1,0:T(8,128)S(1)}, u32[]{:S(2)}, u32[]{:S(2)}) collective-permute-start(f32[1,64,256]{2,1,0:T(8,128)S(1)} %convolution_bitcast_fusion.7), channel_id=1, source_target_pairs={{0,1},{1,0},{2,3},{3,2},{4,5},{5,4},{6,7},{7,6},{8,9},{9,8},{10,11... | collective-permute-start | bytes 196616 | tf_op jit(solution)/shard_map/ppermute | solution.py:26
  94.4 0.4 collective-permute-start.14
  94.8 0.3 fusion.37
  95.1 0.3 fusion.36
  95.4 0.3 convolution_multiply_fusion.8
  95.7 0.9 collective-permute-done.13
  96.9 1.8 %collective-permute-done.14 = f32[1,64,256]{2,1,0:T(8,128)S(1)} collective-permute-done((f32[1,64,256]{2,1,0:T(8,128)S(1)}, f32[1,64,256]{2,1,0:T(8,128)S(1)}, u32[]{:S(2)}, u32[]{:S(2)}) %collective-permute-start.14) | collective-permute-done | bytes 65568 | tf_op jit(solution)/shard_map/ppermute | solution.py:28
  98.7 0.3 convolution_multiply_fusion.6
  99.0 0.3 fusion.58
  100.7 3.8 %collective-permute-start.16 = (f32[1,64,256]{2,1,0:T(8,128)S(1)}, f32[1,64,256]{2,1,0:T(8,128)S(1)}, u32[]{:S(2)}, u32[]{:S(2)}) collective-permute-start(f32[1,64,256]{2,1,0:T(8,128)S(1)} %convolution_bitcast_fusion.4), channel_id=1, source_target_pairs={{8,0},{16,8},{24,16},{0,24},{9,1},{17,9},{25,17},{1,25},{10,2},{18... | collective-permute-start | bytes 196616 | tf_op jit(solution)/shard_map/ppermute | solution.py:28
  104.5 1.7 %collective-permute-start.18 = (f32[1,64,256]{2,1,0:T(8,128)S(1)}, f32[1,64,256]{2,1,0:T(8,128)S(1)}, u32[]{:S(2)}, u32[]{:S(2)}) collective-permute-start(f32[1,64,256]{2,1,0:T(8,128)S(1)} %convolution_bitcast_fusion.2), channel_id=1, source_target_pairs={{2,0},{4,2},{6,4},{0,6},{3,1},{5,3},{7,5},{1,7},{10,8},{12,10},{14... | collective-permute-start | bytes 196616 | tf_op jit(solution)/shard_map/ppermute | solution.py:28
  106.3 1.1 collective-permute-start.19
  107.5 1.0 collective-permute-start.20
  108.6 0.3 fusion.34
  108.9 0.3 fusion.33
  109.2 0.3 convolution_multiply_fusion.2
  109.5 1.7 %collective-permute-done.19 = f32[1,64,256]{2,1,0:T(8,128)S(1)} collective-permute-done((f32[1,64,256]{2,1,0:T(8,128)S(1)}, f32[1,64,256]{2,1,0:T(8,128)S(1)}, u32[]{:S(2)}, u32[]{:S(2)}) %collective-permute-start.19) | collective-permute-done | bytes 65568 | tf_op jit(solution)/shard_map/ppermute | solution.py:26
  111.2 0.3 convolution_multiply_fusion.1
  111.5 0.4 collective-permute-done.20
  111.9 0.3 convolution_multiply_fusion
  112.2 1.0 fusion.54
  (77 shorter events, 9.1 us)
Async XLA Ops:
  0.0 7.2 %collective-permute-start = (f32[8,8,8]{2,1,0:T(8,128)}, f32[8,8,8]{2,1,0:T(8,128)S(1)}, u32[]{:S(2)}, u32[]{:S(2)}) collective-permute-start(f32[8,8,8]{2,1,0:T(8,128)} %param.4), channel_id=1, source_target_pairs={{0,8},{8,16},{16,24},{24,0},{1,9},{9,17},{17,25},{25,1},{2,10},{10... | collective-permute-start | bytes 6152 | tf_op jit(solution)/shard_map/ppermute | solution.py:16
  8.5 3.7 %collective-permute-start.1 = (f32[16,8,8]{2,1,0:T(8,128)S(1)}, f32[16,8,8]{2,1,0:T(8,128)S(1)}, u32[]{:S(2)}, u32[]{:S(2)}) collective-permute-start(f32[16,8,8]{2,1,0:T(8,128)S(1)} %get-tuple-element.9), channel_id=1, source_target_pairs={{0,2},{2,4},{4,6},{6,0},{1,3},{3,5},{5,7},{7,1},{8,10},{10,12},{12... | collective-permute-start | bytes 12296 | tf_op jit(solution)/shard_map/ppermute | solution.py:16
  12.2 41.1 %collective-permute-start.2 = (f32[16,16,8]{2,1,0:T(8,128)S(1)}, f32[16,16,8]{2,1,0:T(8,128)S(1)}, u32[]{:S(2)}, u32[]{:S(2)}) collective-permute-start(f32[16,16,8]{2,1,0:T(8,128)S(1)} %pad_maximum_fusion), channel_id=1, source_target_pairs={{0,1},{1,0},{2,3},{3,2},{4,5},{5,4},{6,7},{7,6},{8,9},{9,8},{10,11... | collective-permute-start | bytes 24584 | tf_op jit(solution)/shard_map/ppermute | solution.py:16
  53.5 7.5 %copy-start.1 = (f32[1,1,1,96,4096]{4,3,2,1,0:T(8,128)S(1)}, f32[1,1,1,96,4096]{4,3,2,1,0:T(8,128)}, u32[]{:S(2)}) copy-start(f32[1,1,1,96,4096]{4,3,2,1,0:T(8,128)} %param.3) | copy-start | bytes 4718596
  69.2 3.3 %copy-start = (f32[1,1,1,96,256]{4,3,2,1,0:T(8,128)S(1)}, f32[1,1,1,96,256]{4,3,2,1,0:T(8,128)}, u32[]{:S(2)}) copy-start(f32[1,1,1,96,256]{4,3,2,1,0:T(8,128)} %param.5) | copy-start | bytes 294916
  73.8 10.0 %collective-permute-start.8 = (f32[1,64,256]{2,1,0:T(8,128)S(1)}, f32[1,64,256]{2,1,0:T(8,128)S(1)}, u32[]{:S(2)}, u32[]{:S(2)}) collective-permute-start(f32[1,64,256]{2,1,0:T(8,128)S(1)} %convolution_bitcast_fusion.12), channel_id=1, source_target_pairs={{1,0},{0,1},{3,2},{2,3},{5,4},{4,5},{7,6},{6,7},{9,8},{8,9},{11,10... | collective-permute-start | bytes 196616 | tf_op jit(solution)/shard_map/ppermute | solution.py:28
  76.3 7.8 %collective-permute-start.7 = (f32[1,64,256]{2,1,0:T(8,128)S(1)}, f32[1,64,256]{2,1,0:T(8,128)S(1)}, u32[]{:S(2)}, u32[]{:S(2)}) collective-permute-start(f32[1,64,256]{2,1,0:T(8,128)S(1)} %convolution_bitcast_fusion.13), channel_id=1, source_target_pairs={{0,1},{1,0},{2,3},{3,2},{4,5},{5,4},{6,7},{7,6},{8,9},{9,8},{10,11... | collective-permute-start | bytes 196616 | tf_op jit(solution)/shard_map/ppermute | solution.py:26
  76.4 6.1 %collective-permute-start.3 = (f32[1,64,256]{2,1,0:T(8,128)S(1)}, f32[1,64,256]{2,1,0:T(8,128)S(1)}, u32[]{:S(2)}, u32[]{:S(2)}) collective-permute-start(f32[1,64,256]{2,1,0:T(8,128)S(1)} %convolution_bitcast_fusion.17), channel_id=1, source_target_pairs={{0,8},{8,16},{16,24},{24,0},{1,9},{9,17},{17,25},{25,1},{2,10},{10... | collective-permute-start | bytes 196616 | tf_op jit(solution)/shard_map/ppermute | solution.py:26
  78.4 6.7 %collective-permute-start.5 = (f32[1,64,256]{2,1,0:T(8,128)S(1)}, f32[1,64,256]{2,1,0:T(8,128)S(1)}, u32[]{:S(2)}, u32[]{:S(2)}) collective-permute-start(f32[1,64,256]{2,1,0:T(8,128)S(1)} %convolution_bitcast_fusion.15), channel_id=1, source_target_pairs={{0,2},{2,4},{4,6},{6,0},{1,3},{3,5},{5,7},{7,1},{8,10},{10,12},{12... | collective-permute-start | bytes 196616 | tf_op jit(solution)/shard_map/ppermute | solution.py:26
  78.4 5.1 %collective-permute-start.4 = (f32[1,64,256]{2,1,0:T(8,128)S(1)}, f32[1,64,256]{2,1,0:T(8,128)S(1)}, u32[]{:S(2)}, u32[]{:S(2)}) collective-permute-start(f32[1,64,256]{2,1,0:T(8,128)S(1)} %convolution_bitcast_fusion.16), channel_id=1, source_target_pairs={{8,0},{16,8},{24,16},{0,24},{9,1},{17,9},{25,17},{1,25},{10,2},{18... | collective-permute-start | bytes 196616 | tf_op jit(solution)/shard_map/ppermute | solution.py:28
  82.5 2.2 %collective-permute-start.6 = (f32[1,64,256]{2,1,0:T(8,128)S(1)}, f32[1,64,256]{2,1,0:T(8,128)S(1)}, u32[]{:S(2)}, u32[]{:S(2)}) collective-permute-start(f32[1,64,256]{2,1,0:T(8,128)S(1)} %convolution_bitcast_fusion.14), channel_id=1, source_target_pairs={{2,0},{4,2},{6,4},{0,6},{3,1},{5,3},{7,5},{1,7},{10,8},{12,10},{14... | collective-permute-start | bytes 196616 | tf_op jit(solution)/shard_map/ppermute | solution.py:28
  86.6 7.8 %collective-permute-start.9 = (f32[1,64,256]{2,1,0:T(8,128)S(1)}, f32[1,64,256]{2,1,0:T(8,128)S(1)}, u32[]{:S(2)}, u32[]{:S(2)}) collective-permute-start(f32[1,64,256]{2,1,0:T(8,128)S(1)} %convolution_bitcast_fusion.11), channel_id=1, source_target_pairs={{0,8},{8,16},{16,24},{24,0},{1,9},{9,17},{17,25},{25,1},{2,10},{10... | collective-permute-start | bytes 196616 | tf_op jit(solution)/shard_map/ppermute | solution.py:26
  86.9 8.2 %collective-permute-start.10 = (f32[1,64,256]{2,1,0:T(8,128)S(1)}, f32[1,64,256]{2,1,0:T(8,128)S(1)}, u32[]{:S(2)}, u32[]{:S(2)}) collective-permute-start(f32[1,64,256]{2,1,0:T(8,128)S(1)} %convolution_bitcast_fusion.10), channel_id=1, source_target_pairs={{8,0},{16,8},{24,16},{0,24},{9,1},{17,9},{25,17},{1,25},{10,2},{18... | collective-permute-start | bytes 196616 | tf_op jit(solution)/shard_map/ppermute | solution.py:28
  90.5 8.5 %collective-permute-start.11 = (f32[1,64,256]{2,1,0:T(8,128)S(1)}, f32[1,64,256]{2,1,0:T(8,128)S(1)}, u32[]{:S(2)}, u32[]{:S(2)}) collective-permute-start(f32[1,64,256]{2,1,0:T(8,128)S(1)} %convolution_bitcast_fusion.9), channel_id=1, source_target_pairs={{0,2},{2,4},{4,6},{6,0},{1,3},{3,5},{5,7},{7,1},{8,10},{10,12},{12... | collective-permute-start | bytes 196616 | tf_op jit(solution)/shard_map/ppermute | solution.py:26
  92.1 3.3 %collective-permute-start.12 = (f32[1,64,256]{2,1,0:T(8,128)S(1)}, f32[1,64,256]{2,1,0:T(8,128)S(1)}, u32[]{:S(2)}, u32[]{:S(2)}) collective-permute-start(f32[1,64,256]{2,1,0:T(8,128)S(1)} %convolution_bitcast_fusion.8), channel_id=1, source_target_pairs={{2,0},{4,2},{6,4},{0,6},{3,1},{5,3},{7,5},{1,7},{10,8},{12,10},{14... | collective-permute-start | bytes 196616 | tf_op jit(solution)/shard_map/ppermute | solution.py:28
  92.3 4.4 %collective-permute-start.13 = (f32[1,64,256]{2,1,0:T(8,128)S(1)}, f32[1,64,256]{2,1,0:T(8,128)S(1)}, u32[]{:S(2)}, u32[]{:S(2)}) collective-permute-start(f32[1,64,256]{2,1,0:T(8,128)S(1)} %convolution_bitcast_fusion.7), channel_id=1, source_target_pairs={{0,1},{1,0},{2,3},{3,2},{4,5},{5,4},{6,7},{7,6},{8,9},{9,8},{10,11... | collective-permute-start | bytes 196616 | tf_op jit(solution)/shard_map/ppermute | solution.py:26
  94.4 4.3 %collective-permute-start.14 = (f32[1,64,256]{2,1,0:T(8,128)S(1)}, f32[1,64,256]{2,1,0:T(8,128)S(1)}, u32[]{:S(2)}, u32[]{:S(2)}) collective-permute-start(f32[1,64,256]{2,1,0:T(8,128)S(1)} %convolution_bitcast_fusion.6), channel_id=1, source_target_pairs={{1,0},{0,1},{3,2},{2,3},{5,4},{4,5},{7,6},{6,7},{9,8},{8,9},{11,10... | collective-permute-start | bytes 196616 | tf_op jit(solution)/shard_map/ppermute | solution.py:28
  100.6 6.9 %collective-permute-start.15 = (f32[1,64,256]{2,1,0:T(8,128)S(1)}, f32[1,64,256]{2,1,0:T(8,128)S(1)}, u32[]{:S(2)}, u32[]{:S(2)}) collective-permute-start(f32[1,64,256]{2,1,0:T(8,128)S(1)} %convolution_bitcast_fusion.5), channel_id=1, source_target_pairs={{0,8},{8,16},{16,24},{24,0},{1,9},{9,17},{17,25},{25,1},{2,10},{10... | collective-permute-start | bytes 196616 | tf_op jit(solution)/shard_map/ppermute | solution.py:26
  100.7 8.2 %collective-permute-start.16 = (f32[1,64,256]{2,1,0:T(8,128)S(1)}, f32[1,64,256]{2,1,0:T(8,128)S(1)}, u32[]{:S(2)}, u32[]{:S(2)}) collective-permute-start(f32[1,64,256]{2,1,0:T(8,128)S(1)} %convolution_bitcast_fusion.4), channel_id=1, source_target_pairs={{8,0},{16,8},{24,16},{0,24},{9,1},{17,9},{25,17},{1,25},{10,2},{18... | collective-permute-start | bytes 196616 | tf_op jit(solution)/shard_map/ppermute | solution.py:28
  104.5 7.7 %collective-permute-start.17 = (f32[1,64,256]{2,1,0:T(8,128)S(1)}, f32[1,64,256]{2,1,0:T(8,128)S(1)}, u32[]{:S(2)}, u32[]{:S(2)}) collective-permute-start(f32[1,64,256]{2,1,0:T(8,128)S(1)} %convolution_bitcast_fusion.3), channel_id=1, source_target_pairs={{0,2},{2,4},{4,6},{6,0},{1,3},{3,5},{5,7},{7,1},{8,10},{10,12},{12... | collective-permute-start | bytes 196616 | tf_op jit(solution)/shard_map/ppermute | solution.py:26
  104.5 4.7 %collective-permute-start.18 = (f32[1,64,256]{2,1,0:T(8,128)S(1)}, f32[1,64,256]{2,1,0:T(8,128)S(1)}, u32[]{:S(2)}, u32[]{:S(2)}) collective-permute-start(f32[1,64,256]{2,1,0:T(8,128)S(1)} %convolution_bitcast_fusion.2), channel_id=1, source_target_pairs={{2,0},{4,2},{6,4},{0,6},{3,1},{5,3},{7,5},{1,7},{10,8},{12,10},{14... | collective-permute-start | bytes 196616 | tf_op jit(solution)/shard_map/ppermute | solution.py:28
  106.3 5.0 %collective-permute-start.19 = (f32[1,64,256]{2,1,0:T(8,128)S(1)}, f32[1,64,256]{2,1,0:T(8,128)S(1)}, u32[]{:S(2)}, u32[]{:S(2)}) collective-permute-start(f32[1,64,256]{2,1,0:T(8,128)S(1)} %convolution_bitcast_fusion.1), channel_id=1, source_target_pairs={{0,1},{1,0},{2,3},{3,2},{4,5},{5,4},{6,7},{7,6},{8,9},{9,8},{10,11... | collective-permute-start | bytes 196616 | tf_op jit(solution)/shard_map/ppermute | solution.py:26
  107.5 4.4 %collective-permute-start.20 = (f32[1,64,256]{2,1,0:T(8,128)S(1)}, f32[1,64,256]{2,1,0:T(8,128)S(1)}, u32[]{:S(2)}, u32[]{:S(2)}) collective-permute-start(f32[1,64,256]{2,1,0:T(8,128)S(1)} %convolution_bitcast_fusion), channel_id=1, source_target_pairs={{1,0},{0,1},{3,2},{2,3},{5,4},{4,5},{7,6},{6,7},{9,8},{8,9},{11,10... | collective-permute-start | bytes 196616 | tf_op jit(solution)/shard_map/ppermute | solution.py:28
where the time goes:
time: 114 us; the launch traced here: 113 us
  blocking collectives  38 us (33%)
  starting transfers between devices  27.3 us (24%)
  matrix products  16.6 us (15%)
  waiting for transfers between devices  14.6 us (13%)
  other arithmetic  10.8 us (9%)
  local copies, waits for them, and re-layouts  3.25 us (3%)
  between operations  2.65 us (2%)
    pmax x1, blocking collectives, per_device(): spectrum_top = 6.0 + lax.pmax(jnp.max(potential), ('gx', 'gy', 'gz'))  38 us
    dot_general x59, matrix products, matmul(): jnp.dot(left, right, precision=lax.Precision.HIGHEST, preferred_element_t...  16.6 us
    ppermute x9, starting transfers between devices, extended(): lax.ppermute(head, axis, [((i + 1) % count, i) for i in range(count)])  15.5 us
    ppermute x3, waiting for transfers between devices, passed_along(): lax.ppermute(shard, axis, [(i, (i + by) % devices) for i in range(devices)])  7.77 us
    div x1, other arithmetic, chebyshev(): current = (operator(initial) - centre * initial) / half_width  7.52 us
    ppermute x9, starting transfers between devices, extended(): lax.ppermute(tail, axis, [(i, (i + 1) % count) for i in range(count)])  6.96 us
    ppermute x3, starting transfers between devices, passed_along(): lax.ppermute(shard, axis, [(i, (i + by) % devices) for i in range(devices)])  4.83 us
    ppermute x9, waiting for transfers between devices, extended(): lax.ppermute(tail, axis, [(i, (i + 1) % count) for i in range(count)])  3.88 us
  transfers between devices with their start and end apart: 21, of which 9 were waited for; matrix products, arithmetic and copies ran while one was open for 5% of the time, Pallas kernels for 0%

commit v1 on v0

v1 whole, which is shorter than its diff:
```python
import functools
import itertools

import jax
import jax.numpy as jnp
from jax import lax
from jax.experimental import pallas as pl
from jax.experimental.pallas import tpu as pltpu
from jax.sharding import PartitionSpec as P

NEWTON = 6
CUTOFF = 1.0
SHIFT = 4.0
AXES = ("gx", "gy", "gz")
MESH = pl.DeviceIdType.MESH
F32 = jnp.float32
BF16 = jnp.bfloat16
NT = (((1,), (1,)), ((), ()))
NN = (((1,), (0,)), ((), ()))


def iota(shape, dim):
    return lax.broadcasted_iota(jnp.int32, shape, dim)


def split(a):
    high = a.astype(BF16)
    return high, (a - high.astype(F32)).astype(BF16)


def dot(a, b, dims=NN):
    return lax.dot_general(a, b, dims, preferred_element_type=F32)


def dot_full(a, b, dims=NN):
    return lax.dot_general(a, b, dims, precision=lax.Precision.HIGHEST, preferred_element_type=F32)


def dot3(a, b, dims=NN):
    return dot(a[0], b[0], dims) + (dot(a[0], b[1], dims) + dot(a[1], b[0], dims))


def dot2(a, b, dims=NN):
    high, low = split(a)
    return dot(high, b, dims) + dot(low, b, dims)


def dot2r(a, b, dims=NN):
    high, low = split(b)
    return dot(a, high, dims) + dot(a, low, dims)


def flag(condition, dtype=F32):
    return jnp.where(condition, 1.0, 0.0).astype(dtype)


def plane_matrix(width):
    cells = width * width
    row, col = iota((cells, cells), 0), iota((cells, cells), 1)
    gap = row - col
    inside = lax.div(row, width) == lax.div(col, width)
    near = ((jnp.abs(gap) == 1) & inside) | (jnp.abs(gap) == width)
    return (jnp.where(gap == 0, 3.0 - SHIFT, 0.0) - 0.5 * flag(near)).astype(BF16)


def kernel(
    length, sizes, orb_hbm, pot_hbm, coef_hbm, out_ref,
    orb, pot, coef, tiles, max1, max2, wide, u, v, rest, facet, ft_in, v_in, p_out, p_in,
    load_sem, tile_send, tile_recv, m1_send, m1_recv, m2_send, m2_recv,
    v_send, v_recv, f_send, f_recv, p_send, p_recv,
):
    me = [lax.axis_index(a) for a in AXES]
    rows, cols = coef.shape
    doubled, area = 2 * length, length * length
    plane, lower = doubled * doubled, length // 2
    half = cols // 2

    def at(offset):
        return tuple(lax.rem(me[k] + (offset[k] % sizes[k]), sizes[k]) for k in range(3))

    def remote(src, dst, send, recv, offset):
        return pltpu.make_async_remote_copy(
            src_ref=src, dst_ref=dst, send_sem=send, recv_sem=recv, device_id=at(offset), device_id_type=MESH
        )

    tile_slots = [s for s in itertools.product((0, 1), repeat=3) if s != (1, 1, 1)]
    tile_to = {s: tuple(1 - k for k in s) for s in tile_slots}
    first = [(d, 0, 0) for d in range(1, sizes[0])]
    second = [(0, b, c) for b in range(sizes[1]) for c in range(sizes[2])][1:]
    faces = []
    for axis in range(3):
        for side in (-1, 1):
            faces.append(tuple(side if k == axis else 0 for k in range(3)))

    def wrapped(offset):
        return tuple(o % n for o, n in zip(offset, sizes))

    greeted = set()
    for offset in list(tile_to.values()) + first + second + faces:
        greeted.add(wrapped(offset))
        greeted.add(wrapped(tuple(-o for o in offset)))
    greeted = sorted(greeted)

    barrier = pltpu.get_barrier_semaphore()
    for offset in greeted:
        pl.semaphore_signal(barrier, inc=1, device_id=at(offset), device_id_type=MESH)

    load_pot = pltpu.make_async_copy(pot_hbm, pot, load_sem.at[0])
    load_orb = pltpu.make_async_copy(
        orb_hbm.at[:, pl.ds((lower - 2) * plane, (length + 4) * plane)], orb, load_sem.at[1]
    )
    load_coef = pltpu.make_async_copy(coef_hbm, coef, load_sem.at[2])
    load_pot.start()
    load_orb.start()
    load_coef.start()

    load_pot.wait()
    lanes = length * doubled
    flat = pot[...].reshape(area, length)
    spread = flag(lax.rem(iota((length, lanes), 1), doubled) == iota((length, lanes), 0))
    keep = lax.div(iota((area, lanes), 1), doubled) == lax.rem(iota((area, lanes), 0), length)
    spread_rows = jnp.where(keep, dot_full(flat, spread), 0.0)
    own = len(tile_slots)
    tiles[own] = jnp.sum(spread_rows.reshape(length, length, lanes), axis=1)
    top = jnp.max(jnp.max(pot[...], axis=0), axis=(0, 1), keepdims=True)
    max1[0] = jnp.broadcast_to(top, max1.shape[1:])

    pl.semaphore_wait(barrier, len(greeted))

    sends = []
    for d, offset in enumerate(first):
        sends.append(remote(max1.at[0], max1.at[d + 1], m1_send.at[d], m1_recv.at[d], offset))
        sends[-1].start()
    tile_copies = []
    for s, slot in enumerate(tile_slots):
        copy = remote(tiles.at[own], tiles.at[s], tile_send.at[s], tile_recv.at[s], tile_to[slot])
        copy.start()
        tile_copies.append(copy)
    m1_copies = list(sends)
    sends += tile_copies

    matrix = plane_matrix(doubled)
    load_orb.wait()

    def w(i):
        return orb[:, pl.ds(i * plane, plane)]

    for i in range(length + 2):
        u[i] = dot2(w(i + 1), matrix) - 0.5 * (w(i) + w(i + 2))

    for copy in m1_copies:
        copy.wait_recv()
    max2[0] = functools.reduce(jnp.maximum, [max1[d] for d in range(sizes[0])])
    m2_copies = []
    for d, offset in enumerate(second):
        copy = remote(max2.at[0], max2.at[d + 1], m2_send.at[d], m2_recv.at[d], offset)
        copy.start()
        m2_copies.append(copy)
    sends += m2_copies

    for copy in tile_copies:
        copy.wait_recv()
    for a in range(2):
        for b in range(2):
            low, high = tiles[4 * a + 2 * b], tiles[4 * a + 2 * b + 1]
            wide[pl.ds(a * length, length), pl.ds(b * lanes, lanes)] = low + pltpu.roll(high, length, 1)

    def potential(x):
        return wide[pl.ds(x, 1), :]

    for i in range(length + 2):
        u[i] = u[i] + potential(i + lower - 1) * w(i + 1)
    for i in range(length):
        centre_plane = u[i + 1]
        v[i] = dot2(centre_plane, matrix) + potential(i + lower) * centre_plane - 0.5 * (u[i] + u[i + 2])

    for copy in m2_copies:
        copy.wait_recv()
    load_coef.wait()
    v_copies = []
    for f, offset in enumerate(faces):
        copy = remote(coef, v_in.at[f ^ 1], v_send.at[f], v_recv.at[f ^ 1], offset)
        copy.start()
        v_copies.append(copy)
    sends += v_copies

    top = functools.reduce(jnp.maximum, [max2[d] for d in range(sizes[1] * sizes[2])])[0:1, 0:1] + 6.0
    centre = (top + CUTOFF) / 2.0
    width = (top - CUTOFF) / 2.0
    away = centre - SHIFT
    alpha = 2.0 / (width * width)
    beta = -2.0 * away * alpha
    gamma = away * away * alpha - 1.0

    source, target = iota((plane, 2 * area), 0), iota((plane, 2 * area), 1)
    inner = lax.rem(target, area)
    wanted = (lower + lax.div(inner, length)) * doubled + lower + lax.rem(inner, length)
    hit = source == wanted
    select = [flag(hit & (lax.div(target, area) == k), BF16) for k in range(2)]

    def filtered(i):
        return alpha * v[i] + beta * u[i + 1] + gamma * w(i + 2)

    own_rows = []
    for pair in range(length // 2):
        rest[:, pl.ds(pair * 2 * area, 2 * area)] = dot2(filtered(2 * pair), select[0]) + dot2(
            filtered(2 * pair + 1), select[1]
        )
        picked = dot_full(wide[pl.ds(lower + 2 * pair, 1), :], select[0].astype(F32)) + dot_full(
            wide[pl.ds(lower + 2 * pair + 1, 1), :], select[1].astype(F32)
        )
        own_rows.append(picked)
    own_potential = jnp.concatenate(own_rows, axis=1)

    r = rest[...]
    gram = dot_full(r, r, NT)
    cells = length * area
    cell = iota((1, cells), 1)
    around = jnp.zeros_like(r)
    for stride in (area, length, 1):
        coordinate = lax.rem(lax.div(cell, stride), length)
        around = around + flag(coordinate > 0) * pltpu.roll(r, stride, 1)
        around = around + flag(coordinate < length - 1) * pltpu.roll(r, cells - stride, 1)
    boxed = (3.0 + own_potential) * r - 0.5 * around
    energy = dot_full(boxed, r, NT)

    face_cell, wanted_row = iota((6 * area, cells), 1), iota((6 * area, 1), 0)
    face, inner = lax.div(wanted_row, area), lax.rem(wanted_row, area)
    major, minor = lax.div(inner, length), lax.rem(inner, length)
    layer = (length - 1) * lax.rem(face, 2)
    axis = lax.div(face, 2)
    picked_cell = jnp.where(
        axis == 0,
        layer * area + inner,
        jnp.where(axis == 1, major * area + layer * length + minor, major * area + minor * length + layer),
    )
    rest_faces = dot2r(flag(face_cell == picked_cell, BF16), r, NT)

    sigma = jnp.sqrt(jnp.sum(jnp.sum(gram * gram, axis=1, keepdims=True), axis=0, keepdims=True))
    eye = flag(iota((rows, rows), 0) == iota((rows, rows), 1))
    product = gram * (1.0 / sigma)
    inverse = None
    for step in range(NEWTON):
        factor = 1.5 * eye - 0.5 * product
        factor_s = split(factor)
        inverse = factor if inverse is None else dot3(factor_s, split(inverse))
        if step < NEWTON - 1:
            once = dot3(split(product), factor_s)
            product = dot3(split(once), factor_s)
    root = inverse * lax.rsqrt(sigma)
    root_s = split(root)

    rest_faces_s = split(rest_faces)
    facet[...] = dot3(rest_faces_s, root_s, NT)
    f_copies = []
    for f, offset in enumerate(faces):
        copy = remote(
            facet.at[pl.ds(f * area, area), :], ft_in.at[pl.ds((f ^ 1) * area, area), :],
            f_send.at[f], f_recv.at[f ^ 1], offset,
        )
        copy.start()
        f_copies.append(copy)
    sends += f_copies

    facet_s = split(facet[...])
    inverse_width = 1.0 / width
    couple = split((-0.5 * inverse_width) * dot3(root_s, rest_faces_s, NT))
    block = dot3(split(dot3(root_s, split(energy))), root_s, NT)
    diagonal = split(inverse_width * (block - centre * eye))

    prior = coef[...]
    current = dot3(diagonal, split(prior))
    carried = [None] * 6
    for f in range(6):
        v_copies[f ^ 1].wait_recv()
        f_copies[f ^ 1].wait_recv()
        carried[f] = dot3(split(ft_in[pl.ds(f * area, area), :]), split(v_in[f]))
    current = current + dot3(couple, split(jnp.concatenate(carried, axis=0)))

    def send_projected(number, part, vectors):
        p_out[number, part] = dot3(facet_s, split(vectors))
        copies = []
        for f, offset in enumerate(faces):
            here, there = pl.ds(f * area, area), pl.ds((f ^ 1) * area, area)
            copy = remote(
                p_out.at[number, part, here, :], p_in.at[number, part, there, :],
                p_send.at[number, part, f], p_recv.at[number, part, f ^ 1], offset,
            )
            copy.start()
            copies.append(copy)
        return copies

    prior = [prior[:, :half], prior[:, half:]]
    current = [current[:, :half], current[:, half:]]
    flying = [send_projected(0, part, current[part]) for part in range(2)]
    for number in range(2):
        following, next_flying = [], []
        for part in range(2):
            mine = 2.0 * dot3(diagonal, split(current[part])) - prior[part]
            for copy in flying[part]:
                copy.wait_recv()
            sends += flying[part]
            mine = mine + 2.0 * dot3(couple, split(p_in[number, part]))
            following.append(mine)
            if number == 0:
                next_flying.append(send_projected(1, part, mine))
            else:
                out_ref[:, pl.ds(part * half, half)] = mine
        prior, current, flying = current, following, next_flying

    for copy in sends:
        copy.wait_send()


def per_device(sizes, orbitals, potential, coefficients):
    length = potential.shape[0]
    rows, cells = orbitals.shape[-2:]
    cols = coefficients.shape[-1]
    doubled, area = 2 * length, length * length
    plane, lanes = doubled * doubled, length * doubled
    others = sizes[1] * sizes[2]
    dma = pltpu.SemaphoreType.DMA
    result = pl.pallas_call(
        functools.partial(kernel, length, sizes),
        out_shape=jax.ShapeDtypeStruct((rows, cols), F32),
        in_specs=[pl.BlockSpec(memory_space=pl.ANY)] * 3,
        out_specs=pl.BlockSpec(memory_space=pltpu.VMEM),
        scratch_shapes=[
            pltpu.VMEM((rows, (length + 4) * plane), F32),
            pltpu.VMEM((length, length, length), F32),
            pltpu.VMEM((rows, cols), F32),
            pltpu.VMEM((8, length, lanes), F32),
            pltpu.VMEM((sizes[0], 8, 128), F32),
            pltpu.VMEM((others, 8, 128), F32),
            pltpu.VMEM((doubled, plane), F32),
            pltpu.VMEM((length + 2, rows, plane), F32),
            pltpu.VMEM((length, rows, plane), F32),
            pltpu.VMEM((rows, length * area), F32),
            pltpu.VMEM((6 * area, rows), F32),
            pltpu.VMEM((6 * area, rows), F32),
            pltpu.VMEM((6, rows, cols), F32),
            pltpu.VMEM((2, 2, 6 * area, cols // 2), F32),
            pltpu.VMEM((2, 2, 6 * area, cols // 2), F32),
            dma((3,)),
            dma((7,)),
            dma((7,)),
            dma((max(sizes[0] - 1, 1),)),
            dma((max(sizes[0] - 1, 1),)),
            dma((max(others - 1, 1),)),
            dma((max(others - 1, 1),)),
            dma((6,)),
            dma((6,)),
            dma((6,)),
            dma((6,)),
            dma((2, 2, 6)),
            dma((2, 2, 6)),
        ],
        compiler_params=pltpu.CompilerParams(
            collective_id=0, has_side_effects=True, vmem_limit_bytes=40 * 1024 * 1024
        ),
    )(orbitals.reshape(rows, cells), potential, coefficients.reshape(rows, cols))
    return result.reshape(coefficients.shape)


def solution(mesh):
    sizes = tuple(mesh.shape[a] for a in AXES)
    placed = (P("gx", "gy", "gz", None, None), P("gx", "gy", "gz"), P("gx", "gy", "gz", None, None))
    return jax.shard_map(
        functools.partial(per_device, sizes),
        mesh=mesh,
        in_specs=placed,
        out_specs=P("gx", "gy", "gz", None, None),
        check_vma=False,
    )
```

time: 114 us -> 37.4 us (0.33)
  blocking collectives: 38 us -> 0 us
  Pallas kernels: 0 us -> 33.5 us
  starting transfers between devices: 27.3 us -> 0 us
  matrix products: 16.6 us -> 0 us
  waiting for transfers between devices: 14.6 us -> 0 us
  other arithmetic: 10.8 us -> 0 us
  between operations: 2.65 us -> 0.01 us
    pmax x1 -> x0, blocking collectives: 38 us -> none  [per_device(): spectrum_top = 6.0 + lax.pmax(jnp.max(potential), ('gx', 'gy', 'gz'))]
    pallas_call x0 -> x1, Pallas kernels: none -> 33.5 us  [per_device(): pl.pallas_call(functools.partial(kernel, length, sizes), out_shape=jax.Sh...]
    ppermute x21 -> x0, starting transfers between devices: 27.3 us -> none  [the longest x9 15.5 us: extended(): lax.ppermute(head, axis, [((i + 1) % count, i) for i in range(count)])]
    dot_general x59 -> x0, matrix products: 16.6 us -> none  [matmul(): jnp.dot(left, right, precision=lax.Precision.HIGHEST, preferred_element_t...]
    ppermute x21 -> x0, waiting for transfers between devices: 14.6 us -> none  [the longest x3 7.77 us: passed_along(): lax.ppermute(shard, axis, [(i, (i + by) % devices) for i in range(devices)])]
    div x1 -> x0, other arithmetic: 7.52 us -> none  [chebyshev(): current = (operator(initial) - centre * initial) / half_width]
    unnamed x5 -> x7, local copies, waits for them, and re-layouts: 0.02 us -> 3.7 us
    sub x1 -> x0, local copies, waits for them, and re-layouts: 1.81 us -> none  [chebyshev(): 2.0 * (operator(current) - centre * current) / half_width - prior_vectors]
  transfers between devices with their start and end apart: 21 -> 0, of which waited for: 9 -> 0; matrix products, arithmetic and copies ran while one was open for 5% -> 0% of each run, Pallas kernels for 0% -> 0%
where the time goes in v1:
time: 37.4 us; the launch traced here: 37.2 us
  Pallas kernels  33.5 us (90%)
  local copies, waits for them, and re-layouts  3.7 us (10%)
    pallas_call x1, Pallas kernels, per_device(): pl.pallas_call(functools.partial(kernel, length, sizes), out_shape=jax.Sh...  33.5 us
    unnamed x7, local copies, waits for them, and re-layouts  3.7 us

profile of v1, /device:TPU:0, one launch (start us, length us, event | category | flops | bytes accessed | tf_op | source)
XLA Modules:
  0.0 37.2 jit_solution(4246566058615108891)
XLA Ops:
  0.0 0.0 copy-start
  0.0 1.4 %copy-done = f32[1,1,1,96,4096]{4,3,2,1,0:T(8,128)S(1)} copy-done((f32[1,1,1,96,4096]{4,3,2,1,0:T(8,128)S(1)}, f32[1,1,1,96,4096]{4,3,2,1,0:T(8,128)}, u32[]{:S(2)}) %copy-start) | copy-done | bytes 1572888
  1.4 0.0 copy-start.1
  1.4 0.9 %copy-done.1 = f32[1,1,1,96,256]{4,3,2,1,0:T(8,128)S(1)} copy-done((f32[1,1,1,96,256]{4,3,2,1,0:T(8,128)S(1)}, f32[1,1,1,96,256]{4,3,2,1,0:T(8,128)}, u32[]{:S(2)}) %copy-start.1) | copy-done | bytes 98328
  2.3 0.0 copy-start.2
  2.3 0.8 %copy-done.2 = f32[8,8,8]{2,1,0:T(8,128)S(1)} copy-done((f32[8,8,8]{2,1,0:T(8,128)S(1)}, f32[8,8,8]{2,1,0:T(8,128)}, u32[]{:S(2)}) %copy-start.2) | copy-done | bytes 2072
  3.1 33.5 %shard_map.37 = f32[96,256]{1,0:T(8,128)S(1)} custom-call(f32[96,4096]{1,0:T(8,128)S(1)} %bitcast.3, f32[8,8,8]{2,1,0:T(8,128)S(1)} %copy-done.2, f32[96,256]{1,0:T(8,128)S(1)} %bitcast.5), custom_call_target="tpu_custom_call" | custom-call | tf_op jit(solution)/shard_map/pallas_call | solution.py:323
  36.5 0.6 %copy.5 = f32[1,1,1,96,256]{4,3,2,1,0:T(8,128)} copy(f32[1,1,1,96,256]{4,3,2,1,0:T(8,128)S(1)} %bitcast.4) | data formatting | bytes 196608
Async XLA Ops:
  0.0 1.4 %copy-start = (f32[1,1,1,96,4096]{4,3,2,1,0:T(8,128)S(1)}, f32[1,1,1,96,4096]{4,3,2,1,0:T(8,128)}, u32[]{:S(2)}) copy-start(f32[1,1,1,96,4096]{4,3,2,1,0:T(8,128)} %param.3) | copy-start | bytes 4718596
  1.4 0.9 %copy-start.1 = (f32[1,1,1,96,256]{4,3,2,1,0:T(8,128)S(1)}, f32[1,1,1,96,256]{4,3,2,1,0:T(8,128)}, u32[]{:S(2)}) copy-start(f32[1,1,1,96,256]{4,3,2,1,0:T(8,128)} %param.5) | copy-start | bytes 294916
  2.3 0.8 %copy-start.2 = (f32[8,8,8]{2,1,0:T(8,128)S(1)}, f32[8,8,8]{2,1,0:T(8,128)}, u32[]{:S(2)}) copy-start(f32[8,8,8]{2,1,0:T(8,128)} %pot_hbm.1) | copy-start | bytes 6148

commit v2 on v1

--- a/solution.py
+++ b/solution.py
@@ -37,12 +37,15 @@
 
 
 def dot3(a, b, dims=NN):
-    return dot(a[0], b[0], dims) + (dot(a[0], b[1], dims) + dot(a[1], b[0], dims))
+    rows = a[0].shape[0]
+    both = dot(jnp.concatenate(a, axis=0), b[0], dims)
+    return both[:rows] + (both[rows:] + dot(a[0], b[1], dims))
 
 
 def dot2(a, b, dims=NN):
-    high, low = split(a)
-    return dot(high, b, dims) + dot(low, b, dims)
+    rows = a.shape[0]
+    both = dot(jnp.concatenate(split(a), axis=0), b, dims)
+    return both[:rows] + both[rows:]
 
 
 def dot2r(a, b, dims=NN):
@@ -65,7 +68,7 @@
 
 def kernel(
     length, sizes, orb_hbm, pot_hbm, coef_hbm, out_ref,
-    orb, pot, coef, tiles, max1, max2, wide, u, v, rest, facet, ft_in, v_in, p_out, p_in,
+    matrix, select, pick, orb, pot, coef, tiles, max1, max2, wide, u, v, rest, facet, ft_in, v_in, p_out, p_in,
     load_sem, tile_send, tile_recv, m1_send, m1_recv, m2_send, m2_recv,
     v_send, v_recv, f_send, f_recv, p_send, p_recv,
 ):
@@ -113,6 +116,23 @@
     load_pot.start()
     load_orb.start()
     load_coef.start()
+
+    matrix[...] = plane_matrix(doubled)
+    source, target = iota((plane, 2 * area), 0), iota((plane, 2 * area), 1)
+    inner = lax.rem(target, area)
+    wanted = (lower + lax.div(inner, length)) * doubled + lower + lax.rem(inner, length)
+    for k in range(2):
+        select[k] = flag((source == wanted) & (lax.div(target, area) == k), BF16)
+    cells = length * area
+    cell = iota((1, cells), 1)
+    for f in range(6):
+        inner = iota((area, 1), 0)
+        major, minor = lax.div(inner, length), lax.rem(inner, length)
+        layer = (length - 1) * (f % 2)
+        picked_cell = (
+            layer * area + inner, major * area + layer * length + minor, major * area + minor * length + layer
+        )[f // 2]
+        pick[pl.ds(f * area, area), :] = flag(iota((area, cells), 1) == picked_cell, BF16)
 
     load_pot.wait()
     lanes = length * doubled
@@ -139,14 +159,22 @@
     m1_copies = list(sends)
     sends += tile_copies
 
-    matrix = plane_matrix(doubled)
+    load_coef.wait()
+    v_copies = {}
+    shared = [f for f in range(6) if f % 2 == 0 or sizes[f // 2] > 2]
+    for f in shared:
+        v_copies[f] = remote(coef, v_in.at[f ^ 1], v_send.at[f], v_recv.at[f ^ 1], faces[f])
+    for f in shared[:2]:
+        v_copies[f].start()
+    sends += v_copies.values()
+
     load_orb.wait()
 
     def w(i):
         return orb[:, pl.ds(i * plane, plane)]
 
     for i in range(length + 2):
-        u[i] = dot2(w(i + 1), matrix) - 0.5 * (w(i) + w(i + 2))
+        u[i] = dot2(w(i + 1), matrix[...]) - 0.5 * (w(i) + w(i + 2))
 
     for copy in m1_copies:
         copy.wait_recv()
@@ -172,17 +200,12 @@
         u[i] = u[i] + potential(i + lower - 1) * w(i + 1)
     for i in range(length):
         centre_plane = u[i + 1]
-        v[i] = dot2(centre_plane, matrix) + potential(i + lower) * centre_plane - 0.5 * (u[i] + u[i + 2])
+        v[i] = dot2(centre_plane, matrix[...]) + potential(i + lower) * centre_plane - 0.5 * (u[i] + u[i + 2])
 
     for copy in m2_copies:
         copy.wait_recv()
-    load_coef.wait()
-    v_copies = []
-    for f, offset in enumerate(faces):
-        copy = remote(coef, v_in.at[f ^ 1], v_send.at[f], v_recv.at[f ^ 1], offset)
-        copy.start()
-        v_copies.append(copy)
-    sends += v_copies
+    for f in shared[2:]:
+        v_copies[f].start()
 
     top = functools.reduce(jnp.maximum, [max2[d] for d in range(sizes[1] * sizes[2])])[0:1, 0:1] + 6.0
     centre = (top + CUTOFF) / 2.0
@@ -191,12 +214,6 @@
     alpha = 2.0 / (width * width)
     beta = -2.0 * away * alpha
     gamma = away * away * alpha - 1.0
-
-    source, target = iota((plane, 2 * area), 0), iota((plane, 2 * area), 1)
-    inner = lax.rem(target, area)
-    wanted = (lower + lax.div(inner, length)) * doubled + lower + lax.rem(inner, length)
-    hit = source == wanted
-    select = [flag(hit & (lax.div(target, area) == k), BF16) for k in range(2)]
 
     def filtered(i):
         return alpha * v[i] + beta * u[i + 1] + gamma * w(i + 2)
@@ -214,33 +231,16 @@
 
     r = rest[...]
     gram = dot_full(r, r, NT)
-    cells = length * area
-    cell = iota((1, cells), 1)
-    around = jnp.zeros_like(r)
-    for stride in (area, length, 1):
-        coordinate = lax.rem(lax.div(cell, stride), length)
-        around = around + flag(coordinate > 0) * pltpu.roll(r, stride, 1)
-        around = around + flag(coordinate < length - 1) * pltpu.roll(r, cells - stride, 1)
-    boxed = (3.0 + own_potential) * r - 0.5 * around
-    energy = dot_full(boxed, r, NT)
-
-    face_cell, wanted_row = iota((6 * area, cells), 1), iota((6 * area, 1), 0)
-    face, inner = lax.div(wanted_row, area), lax.rem(wanted_row, area)
-    major, minor = lax.div(inner, length), lax.rem(inner, length)
-    layer = (length - 1) * lax.rem(face, 2)
-    axis = lax.div(face, 2)
-    picked_cell = jnp.where(
-        axis == 0,
-        layer * area + inner,
-        jnp.where(axis == 1, major * area + layer * length + minor, major * area + minor * length + layer),
-    )
-    rest_faces = dot2r(flag(face_cell == picked_cell, BF16), r, NT)
-
     sigma = jnp.sqrt(jnp.sum(jnp.sum(gram * gram, axis=1, keepdims=True), axis=0, keepdims=True))
     eye = flag(iota((rows, rows), 0) == iota((rows, rows), 1))
     product = gram * (1.0 / sigma)
     inverse = None
+    r_s = split(r)
+    rest_faces = []
     for step in range(NEWTON):
+        for f in range(6 * step // NEWTON, 6 * (step + 1) // NEWTON):
+            here = pick[pl.ds(f * area, area), :]
+            rest_faces.append(dot(here, r_s[0], NT) + dot(here, r_s[1], NT))
         factor = 1.5 * eye - 0.5 * product
         factor_s = split(factor)
         inverse = factor if inverse is None else dot3(factor_s, split(inverse))
@@ -250,7 +250,7 @@
     root = inverse * lax.rsqrt(sigma)
     root_s = split(root)
 
-    rest_faces_s = split(rest_faces)
+    rest_faces_s = split(jnp.concatenate(rest_faces, axis=0))
     facet[...] = dot3(rest_faces_s, root_s, NT)
     f_copies = []
     for f, offset in enumerate(faces):
@@ -265,16 +265,25 @@
     facet_s = split(facet[...])
     inverse_width = 1.0 / width
     couple = split((-0.5 * inverse_width) * dot3(root_s, rest_faces_s, NT))
+    around = jnp.zeros_like(r)
+    for stride in (area, length, 1):
+        coordinate = lax.rem(lax.div(cell, stride), length)
+        around = around + flag(coordinate > 0) * pltpu.roll(r, stride, 1)
+        around = around + flag(coordinate < length - 1) * pltpu.roll(r, cells - stride, 1)
+    boxed = (3.0 + own_potential) * r - 0.5 * around
+    energy = dot3(split(boxed), r_s, NT)
     block = dot3(split(dot3(root_s, split(energy))), root_s, NT)
     diagonal = split(inverse_width * (block - centre * eye))
 
     prior = coef[...]
     current = dot3(diagonal, split(prior))
-    carried = [None] * 6
+    for copy in v_copies.values():
+        copy.wait_recv()
+    came = [split(v_in[f if f ^ 1 in shared else f ^ 1]) for f in range(6)]
+    carried = []
     for f in range(6):
-        v_copies[f ^ 1].wait_recv()
         f_copies[f ^ 1].wait_recv()
-        carried[f] = dot3(split(ft_in[pl.ds(f * area, area), :]), split(v_in[f]))
+        carried.append(dot3(split(ft_in[pl.ds(f * area, area), :]), came[f]))
     current = current + dot3(couple, split(jnp.concatenate(carried, axis=0)))
 
     def send_projected(number, part, vectors):
@@ -323,9 +332,12 @@
     result = pl.pallas_call(
         functools.partial(kernel, length, sizes),
         out_shape=jax.ShapeDtypeStruct((rows, cols), F32),
-        in_specs=[pl.BlockSpec(memory_space=pl.ANY)] * 3,
+        in_specs=[pl.BlockSpec(memory_space=pltpu.HBM)] * 3,
         out_specs=pl.BlockSpec(memory_space=pltpu.VMEM),
         scratch_shapes=[
+            pltpu.VMEM((plane, plane), BF16),
+            pltpu.VMEM((2, plane, 2 * area), BF16),
+            pltpu.VMEM((6 * area, length * area), BF16),
             pltpu.VMEM((rows, (length + 4) * plane), F32),
             pltpu.VMEM((length, length, length), F32),
             pltpu.VMEM((rows, cols), F32),
@@ -356,7 +368,7 @@
             dma((2, 2, 6)),
         ],
         compiler_params=pltpu.CompilerParams(
-            collective_id=0, has_side_effects=True, vmem_limit_bytes=40 * 1024 * 1024
+            collective_id=0, has_side_effects=True, vmem_limit_bytes=60 * 1024 * 1024
         ),
     )(orbitals.reshape(rows, cells), potential, coefficients.reshape(rows, cols))
     return result.reshape(coefficients.shape)

time: 37.4 us -> 35.1 us (0.939)
  local copies, waits for them, and re-layouts: 3.7 us -> 1.54 us
    unnamed x7 -> x1, local copies, waits for them, and re-layouts: 3.7 us -> 1.54 us
where the time goes in v2:
time: 35.1 us; the launch traced here: 34.9 us
  Pallas kernels  33.4 us (95%)
  local copies, waits for them, and re-layouts  1.54 us (4%)
    pallas_call x1, Pallas kernels, per_device(): pl.pallas_call(functools.partial(kernel, length, sizes), out_shape=jax.Sh...  33.4 us
    unnamed x1, local copies, waits for them, and re-layouts  1.54 us

profile of v2, /device:TPU:0, one launch (start us, length us, event | category | flops | bytes accessed | tf_op | source)
XLA Modules:
  0.0 34.9 jit_solution(12777616994064972755)
XLA Ops:
  0.0 33.4 %shard_map.37 = f32[96,256]{1,0:T(8,128)} custom-call(f32[96,4096]{1,0:T(8,128)} %bitcast.3, f32[8,8,8]{2,1,0:T(8,128)} %pot_hbm.1, f32[96,256]{1,0:T(8,128)} %bitcast.5), custom_call_target="tpu_custom_call" | custom-call | tf_op jit(solution)/shard_map/pallas_call | solution.py:332
  33.4 1.5 %copy.5 = f32[1,1,1,96,256]{4,3,2,1,0:T(8,128)} copy(f32[1,1,1,96,256]{4,3,2,1,0:T(8,128)} %bitcast.4) | data formatting | bytes 196608

commit v3 on v2

--- a/solution.py
+++ b/solution.py
@@ -9,6 +9,7 @@
 from jax.sharding import PartitionSpec as P
 
 NEWTON = 6
+PARTS = 1
 CUTOFF = 1.0
 SHIFT = 4.0
 AXES = ("gx", "gy", "gz")
@@ -59,7 +60,7 @@
 
 def plane_matrix(width):
     cells = width * width
-    row, col = iota((cells, cells), 0), iota((cells, cells), 1)
+    row, col = iota((cells, 1), 0), iota((1, cells), 1)
     gap = row - col
     inside = lax.div(row, width) == lax.div(col, width)
     near = ((jnp.abs(gap) == 1) & inside) | (jnp.abs(gap) == width)
@@ -76,7 +77,7 @@
     rows, cols = coef.shape
     doubled, area = 2 * length, length * length
     plane, lower = doubled * doubled, length // 2
-    half = cols // 2
+    half = cols // PARTS
 
     def at(offset):
         return tuple(lax.rem(me[k] + (offset[k] % sizes[k]), sizes[k]) for k in range(3))
@@ -118,11 +119,11 @@
     load_coef.start()
 
     matrix[...] = plane_matrix(doubled)
-    source, target = iota((plane, 2 * area), 0), iota((plane, 2 * area), 1)
+    source, target = iota((plane, 1), 0), iota((1, 2 * area), 1)
     inner = lax.rem(target, area)
     wanted = (lower + lax.div(inner, length)) * doubled + lower + lax.rem(inner, length)
     for k in range(2):
-        select[k] = flag((source == wanted) & (lax.div(target, area) == k), BF16)
+        select[k] = flag(source == jnp.where(lax.div(target, area) == k, wanted, -1), BF16)
     cells = length * area
     cell = iota((1, cells), 1)
     for f in range(6):
@@ -132,13 +133,13 @@
         picked_cell = (
             layer * area + inner, major * area + layer * length + minor, major * area + minor * length + layer
         )[f // 2]
-        pick[pl.ds(f * area, area), :] = flag(iota((area, cells), 1) == picked_cell, BF16)
+        pick[pl.ds(f * area, area), :] = flag(cell == picked_cell, BF16)
 
     load_pot.wait()
     lanes = length * doubled
     flat = pot[...].reshape(area, length)
-    spread = flag(lax.rem(iota((length, lanes), 1), doubled) == iota((length, lanes), 0))
-    keep = lax.div(iota((area, lanes), 1), doubled) == lax.rem(iota((area, lanes), 0), length)
+    spread = flag(lax.rem(iota((1, lanes), 1), doubled) == iota((length, 1), 0))
+    keep = lax.div(iota((1, lanes), 1), doubled) == lax.rem(iota((area, 1), 0), length)
     spread_rows = jnp.where(keep, dot_full(flat, spread), 0.0)
     own = len(tile_slots)
     tiles[own] = jnp.sum(spread_rows.reshape(length, length, lanes), axis=1)
@@ -253,18 +254,26 @@
     rest_faces_s = split(jnp.concatenate(rest_faces, axis=0))
     facet[...] = dot3(rest_faces_s, root_s, NT)
     f_copies = []
+    face_copies = []
     for f, offset in enumerate(faces):
-        copy = remote(
-            facet.at[pl.ds(f * area, area), :], ft_in.at[pl.ds((f ^ 1) * area, area), :],
-            f_send.at[f], f_recv.at[f ^ 1], offset,
-        )
+        if sizes[f // 2] > 2:
+            face_copies.append((f, pl.ds(f * area, area), pl.ds((f ^ 1) * area, area), offset))
+        elif f % 2 == 0:
+            both = pl.ds(f * area, 2 * area)
+            face_copies.append((f, both, both, offset))
+    for f, here, there, offset in face_copies:
+        copy = remote(facet.at[here, :], ft_in.at[there, :], f_send.at[f], f_recv.at[f], offset)
         copy.start()
         f_copies.append(copy)
     sends += f_copies
 
     facet_s = split(facet[...])
     inverse_width = 1.0 / width
-    couple = split((-0.5 * inverse_width) * dot3(root_s, rest_faces_s, NT))
+    slots = []
+    for f in range(6):
+        slots.append(rest_faces[f if sizes[f // 2] > 2 else f ^ 1])
+    slots_s = split(jnp.concatenate(slots, axis=0))
+    couple = split((-0.5 * inverse_width) * dot3(root_s, slots_s, NT))
     around = jnp.zeros_like(r)
     for stride in (area, length, 1):
         coordinate = lax.rem(lax.div(cell, stride), length)
@@ -281,30 +290,30 @@
         copy.wait_recv()
     came = [split(v_in[f if f ^ 1 in shared else f ^ 1]) for f in range(6)]
     carried = []
+    for copy in f_copies:
+        copy.wait_recv()
     for f in range(6):
-        f_copies[f ^ 1].wait_recv()
         carried.append(dot3(split(ft_in[pl.ds(f * area, area), :]), came[f]))
     current = current + dot3(couple, split(jnp.concatenate(carried, axis=0)))
 
     def send_projected(number, part, vectors):
         p_out[number, part] = dot3(facet_s, split(vectors))
         copies = []
-        for f, offset in enumerate(faces):
-            here, there = pl.ds(f * area, area), pl.ds((f ^ 1) * area, area)
+        for f, here, there, offset in face_copies:
             copy = remote(
                 p_out.at[number, part, here, :], p_in.at[number, part, there, :],
-                p_send.at[number, part, f], p_recv.at[number, part, f ^ 1], offset,
+                p_send.at[number, part, f], p_recv.at[number, part, f], offset,
             )
             copy.start()
             copies.append(copy)
         return copies
 
-    prior = [prior[:, :half], prior[:, half:]]
-    current = [current[:, :half], current[:, half:]]
-    flying = [send_projected(0, part, current[part]) for part in range(2)]
+    prior = [prior[:, k * half : (k + 1) * half] for k in range(PARTS)]
+    current = [current[:, k * half : (k + 1) * half] for k in range(PARTS)]
+    flying = [send_projected(0, part, current[part]) for part in range(PARTS)]
     for number in range(2):
         following, next_flying = [], []
-        for part in range(2):
+        for part in range(PARTS):
             mine = 2.0 * dot3(diagonal, split(current[part])) - prior[part]
             for copy in flying[part]:
                 copy.wait_recv()
@@ -351,8 +360,8 @@
             pltpu.VMEM((6 * area, rows), F32),
             pltpu.VMEM((6 * area, rows), F32),
             pltpu.VMEM((6, rows, cols), F32),
-            pltpu.VMEM((2, 2, 6 * area, cols // 2), F32),
-            pltpu.VMEM((2, 2, 6 * area, cols // 2), F32),
+            pltpu.VMEM((2, PARTS, 6 * area, cols // PARTS), F32),
+            pltpu.VMEM((2, PARTS, 6 * area, cols // PARTS), F32),
             dma((3,)),
             dma((7,)),
             dma((7,)),
@@ -364,8 +373,8 @@
             dma((6,)),
             dma((6,)),
             dma((6,)),
-            dma((2, 2, 6)),
-            dma((2, 2, 6)),
+            dma((2, PARTS, 6)),
+            dma((2, PARTS, 6)),
         ],
         compiler_params=pltpu.CompilerParams(
             collective_id=0, has_side_effects=True, vmem_limit_bytes=60 * 1024 * 1024

time: 35.1 us -> 34.8 us (level)
  no operation moved by 1% of the time
where the time goes in v3:
time: 34.8 us; the launch traced here: 34.6 us
  Pallas kernels  33.1 us (95%)
  local copies, waits for them, and re-layouts  1.54 us (4%)
    pallas_call x1, Pallas kernels, per_device(): pl.pallas_call(functools.partial(kernel, length, sizes), out_shape=jax.Sh...  33.1 us
    unnamed x1, local copies, waits for them, and re-layouts  1.54 us

profile of v3, /device:TPU:0, one launch (start us, length us, event | category | flops | bytes accessed | tf_op | source)
XLA Modules:
  0.0 34.6 jit_solution(10014042120775508158)
XLA Ops:
  0.0 33.1 %shard_map.37 = f32[96,256]{1,0:T(8,128)} custom-call(f32[96,4096]{1,0:T(8,128)} %bitcast.3, f32[8,8,8]{2,1,0:T(8,128)} %pot_hbm.1, f32[96,256]{1,0:T(8,128)} %bitcast.5), custom_call_target="tpu_custom_call" | custom-call | tf_op jit(solution)/shard_map/pallas_call | solution.py:341
  33.1 1.5 %copy.5 = f32[1,1,1,96,256]{4,3,2,1,0:T(8,128)} copy(f32[1,1,1,96,256]{4,3,2,1,0:T(8,128)} %bitcast.4) | data formatting | bytes 196608

commit v4 on v3

--- a/solution.py
+++ b/solution.py
@@ -69,7 +69,7 @@
 
 def kernel(
     length, sizes, orb_hbm, pot_hbm, coef_hbm, out_ref,
-    matrix, select, pick, orb, pot, coef, tiles, max1, max2, wide, u, v, rest, facet, ft_in, v_in, p_out, p_in,
+    matrix, select, pick, orb, pot, coef, tiles, max1, max2, wide, u, v, rest, rest_faces, facet, ft_in, v_in, p_out, p_in,
     load_sem, tile_send, tile_recv, m1_send, m1_recv, m2_send, m2_recv,
     v_send, v_recv, f_send, f_recv, p_send, p_recv,
 ):
@@ -172,9 +172,10 @@
     load_orb.wait()
 
     def w(i):
-        return orb[:, pl.ds(i * plane, plane)]
-
-    for i in range(length + 2):
+        return orb[:, pl.ds(pl.multiple_of(i * plane, plane), plane)]
+
+    @pl.loop(0, length + 2, unroll=2)
+    def _(i):
         u[i] = dot2(w(i + 1), matrix[...]) - 0.5 * (w(i) + w(i + 2))
 
     for copy in m1_copies:
@@ -197,9 +198,12 @@
     def potential(x):
         return wide[pl.ds(x, 1), :]
 
-    for i in range(length + 2):
+    @pl.loop(0, length + 2)
+    def _(i):
         u[i] = u[i] + potential(i + lower - 1) * w(i + 1)
-    for i in range(length):
+
+    @pl.loop(0, length, unroll=2)
+    def _(i):
         centre_plane = u[i + 1]
         v[i] = dot2(centre_plane, matrix[...]) + potential(i + lower) * centre_plane - 0.5 * (u[i] + u[i + 2])
 
@@ -219,39 +223,39 @@
     def filtered(i):
         return alpha * v[i] + beta * u[i + 1] + gamma * w(i + 2)
 
-    own_rows = []
-    for pair in range(length // 2):
-        rest[:, pl.ds(pair * 2 * area, 2 * area)] = dot2(filtered(2 * pair), select[0]) + dot2(
-            filtered(2 * pair + 1), select[1]
-        )
-        picked = dot_full(wide[pl.ds(lower + 2 * pair, 1), :], select[0].astype(F32)) + dot_full(
-            wide[pl.ds(lower + 2 * pair + 1, 1), :], select[1].astype(F32)
-        )
-        own_rows.append(picked)
-    own_potential = jnp.concatenate(own_rows, axis=1)
+    @pl.loop(0, length // 2)
+    def _(pair):
+        here = pl.ds(pl.multiple_of(pair * 2 * area, 2 * area), 2 * area)
+        rest[:, here] = dot2(filtered(2 * pair), select[0]) + dot2(filtered(2 * pair + 1), select[1])
 
     r = rest[...]
-    gram = dot_full(r, r, NT)
+    r_s = split(r)
+    gram = dot3(r_s, r_s, NT)
     sigma = jnp.sqrt(jnp.sum(jnp.sum(gram * gram, axis=1, keepdims=True), axis=0, keepdims=True))
     eye = flag(iota((rows, rows), 0) == iota((rows, rows), 1))
     product = gram * (1.0 / sigma)
-    inverse = None
-    r_s = split(r)
-    rest_faces = []
-    for step in range(NEWTON):
-        for f in range(6 * step // NEWTON, 6 * (step + 1) // NEWTON):
-            here = pick[pl.ds(f * area, area), :]
-            rest_faces.append(dot(here, r_s[0], NT) + dot(here, r_s[1], NT))
+
+    def pick_face(f):
+        here = pl.ds(pl.multiple_of(f * area, area), area)
+        rest_faces[here, :] = dot(pick[here, :], r_s[0], NT) + dot(pick[here, :], r_s[1], NT)
+
+    def newton(step, state):
+        product, inverse = state
         factor = 1.5 * eye - 0.5 * product
         factor_s = split(factor)
-        inverse = factor if inverse is None else dot3(factor_s, split(inverse))
-        if step < NEWTON - 1:
-            once = dot3(split(product), factor_s)
-            product = dot3(split(once), factor_s)
+        once = dot3(split(product), factor_s)
+        inverse = dot3(split(inverse), factor_s)
+        pick_face(step)
+        return dot3(split(once), factor_s), inverse
+
+    product, inverse = lax.fori_loop(0, NEWTON - 1, newton, (product, eye))
+    for f in range(NEWTON - 1, 6):
+        pick_face(f)
+    inverse = dot3(split(inverse), split(1.5 * eye - 0.5 * product))
     root = inverse * lax.rsqrt(sigma)
     root_s = split(root)
 
-    rest_faces_s = split(jnp.concatenate(rest_faces, axis=0))
+    rest_faces_s = split(rest_faces[...])
     facet[...] = dot3(rest_faces_s, root_s, NT)
     f_copies = []
     face_copies = []
@@ -271,9 +275,14 @@
     inverse_width = 1.0 / width
     slots = []
     for f in range(6):
-        slots.append(rest_faces[f if sizes[f // 2] > 2 else f ^ 1])
+        slots.append(rest_faces[pl.ds((f if sizes[f // 2] > 2 else f ^ 1) * area, area), :])
     slots_s = split(jnp.concatenate(slots, axis=0))
     couple = split((-0.5 * inverse_width) * dot3(root_s, slots_s, NT))
+    own_wide = dot2(wide[pl.ds(lower, length), :], select[0])
+    own_odd = pltpu.roll(own_wide, area, 1)
+    own_potential = jnp.concatenate(
+        [own_wide[k : k + 1, :] + own_odd[k + 1 : k + 2, :] for k in range(0, length, 2)], axis=1
+    )
     around = jnp.zeros_like(r)
     for stride in (area, length, 1):
         coordinate = lax.rem(lax.div(cell, stride), length)
@@ -359,6 +368,7 @@
             pltpu.VMEM((rows, length * area), F32),
             pltpu.VMEM((6 * area, rows), F32),
             pltpu.VMEM((6 * area, rows), F32),
+            pltpu.VMEM((6 * area, rows), F32),
             pltpu.VMEM((6, rows, cols), F32),
             pltpu.VMEM((2, PARTS, 6 * area, cols // PARTS), F32),
             pltpu.VMEM((2, PARTS, 6 * area, cols // PARTS), F32),

time: 34.8 us -> 34.6 us (level)
  no operation moved by 1% of the time
where the time goes in v4:
time: 34.6 us; the launch traced here: 34.4 us
  Pallas kernels  32.9 us (95%)
  local copies, waits for them, and re-layouts  1.54 us (4%)
    pallas_call x1, Pallas kernels, per_device(): pl.pallas_call(functools.partial(kernel, length, sizes), out_shape=jax.Sh...  32.9 us
    unnamed x1, local copies, waits for them, and re-layouts  1.54 us

profile of v4, /device:TPU:0, one launch (start us, length us, event | category | flops | bytes accessed | tf_op | source)
XLA Modules:
  0.0 34.4 jit_solution(2852750574995122534)
XLA Ops:
  0.0 32.9 %shard_map.37 = f32[96,256]{1,0:T(8,128)} custom-call(f32[96,4096]{1,0:T(8,128)} %bitcast.3, f32[8,8,8]{2,1,0:T(8,128)} %pot_hbm.1, f32[96,256]{1,0:T(8,128)} %bitcast.5), custom_call_target="tpu_custom_call" | custom-call | tf_op jit(solution)/shard_map/pallas_call | solution.py:350
  32.9 1.5 %copy.5 = f32[1,1,1,96,256]{4,3,2,1,0:T(8,128)} copy(f32[1,1,1,96,256]{4,3,2,1,0:T(8,128)} %bitcast.4) | data formatting | bytes 196608

commit v5 on v4

--- a/solution.py
+++ b/solution.py
@@ -9,7 +9,7 @@
 from jax.sharding import PartitionSpec as P
 
 NEWTON = 6
-PARTS = 1
+PARTS = 2
 CUTOFF = 1.0
 SHIFT = 4.0
 AXES = ("gx", "gy", "gz")
@@ -67,10 +67,22 @@
     return (jnp.where(gap == 0, 3.0 - SHIFT, 0.0) - 0.5 * flag(near)).astype(BF16)
 
 
+def max_stages(sizes):
+    reach = [range(0, n, 2) for n in sizes]
+    every = [o for o in itertools.product(*reach) if any(o)]
+    if len(every) < 8:
+        return [every]
+    stages = []
+    for axis in range(3):
+        if len(reach[axis]) > 1:
+            stages.append([tuple(d if k == axis else 0 for k in range(3)) for d in reach[axis][1:]])
+    return stages
+
+
 def kernel(
     length, sizes, orb_hbm, pot_hbm, coef_hbm, out_ref,
-    matrix, select, pick, orb, pot, coef, tiles, max1, max2, wide, u, v, rest, rest_faces, facet, ft_in, v_in, p_out, p_in,
-    load_sem, tile_send, tile_recv, m1_send, m1_recv, m2_send, m2_recv,
+    matrix, select, pick, orb, pot, coef, tiles, tops, tops_in, wide, u, v, own_w, own_u, own_v, rest_faces, facet, ft_in, v_in, p_out, p_in,
+    load_sem, tile_send, tile_recv, top_send, top_recv,
     v_send, v_recv, f_send, f_recv, p_send, p_recv,
 ):
     me = [lax.axis_index(a) for a in AXES]
@@ -89,8 +101,7 @@
 
     tile_slots = [s for s in itertools.product((0, 1), repeat=3) if s != (1, 1, 1)]
     tile_to = {s: tuple(1 - k for k in s) for s in tile_slots}
-    first = [(d, 0, 0) for d in range(1, sizes[0])]
-    second = [(0, b, c) for b in range(sizes[1]) for c in range(sizes[2])][1:]
+    stages = max_stages(sizes)
     faces = []
     for axis in range(3):
         for side in (-1, 1):
@@ -100,7 +111,7 @@
         return tuple(o % n for o, n in zip(offset, sizes))
 
     greeted = set()
-    for offset in list(tile_to.values()) + first + second + faces:
+    for offset in list(tile_to.values()) + sum(stages, []) + faces:
         greeted.add(wrapped(offset))
         greeted.add(wrapped(tuple(-o for o in offset)))
     greeted = sorted(greeted)
@@ -143,21 +154,15 @@
     spread_rows = jnp.where(keep, dot_full(flat, spread), 0.0)
     own = len(tile_slots)
     tiles[own] = jnp.sum(spread_rows.reshape(length, length, lanes), axis=1)
-    top = jnp.max(jnp.max(pot[...], axis=0), axis=(0, 1), keepdims=True)
-    max1[0] = jnp.broadcast_to(top, max1.shape[1:])
 
     pl.semaphore_wait(barrier, len(greeted))
 
     sends = []
-    for d, offset in enumerate(first):
-        sends.append(remote(max1.at[0], max1.at[d + 1], m1_send.at[d], m1_recv.at[d], offset))
-        sends[-1].start()
     tile_copies = []
     for s, slot in enumerate(tile_slots):
         copy = remote(tiles.at[own], tiles.at[s], tile_send.at[s], tile_recv.at[s], tile_to[slot])
         copy.start()
         tile_copies.append(copy)
-    m1_copies = list(sends)
     sends += tile_copies
 
     load_coef.wait()
@@ -174,19 +179,19 @@
     def w(i):
         return orb[:, pl.ds(pl.multiple_of(i * plane, plane), plane)]
 
+    def pair_lanes(pair):
+        return pl.ds(pl.multiple_of(pair * 2 * area, 2 * area), 2 * area)
+
+    def own_cells(even, odd):
+        return dot2(even, select[0]) + dot2(odd, select[1])
+
     @pl.loop(0, length + 2, unroll=2)
     def _(i):
         u[i] = dot2(w(i + 1), matrix[...]) - 0.5 * (w(i) + w(i + 2))
 
-    for copy in m1_copies:
-        copy.wait_recv()
-    max2[0] = functools.reduce(jnp.maximum, [max1[d] for d in range(sizes[0])])
-    m2_copies = []
-    for d, offset in enumerate(second):
-        copy = remote(max2.at[0], max2.at[d + 1], m2_send.at[d], m2_recv.at[d], offset)
-        copy.start()
-        m2_copies.append(copy)
-    sends += m2_copies
+    @pl.loop(0, length // 2)
+    def _(pair):
+        own_w[:, pair_lanes(pair)] = own_cells(w(2 * pair + 2), w(2 * pair + 3))
 
     for copy in tile_copies:
         copy.wait_recv()
@@ -195,6 +200,32 @@
             low, high = tiles[4 * a + 2 * b], tiles[4 * a + 2 * b + 1]
             wide[pl.ds(a * length, length), pl.ds(b * lanes, lanes)] = low + pltpu.roll(high, length, 1)
 
+    sent = 0
+    flying = []
+
+    def send_max(stage):
+        copies = []
+        for d, offset in enumerate(stages[stage]):
+            k = sent + d
+            copy = remote(
+                tops.at[stage], tops_in.at[k], top_send.at[k], top_recv.at[k], offset
+            )
+            copy.start()
+            copies.append(copy)
+        return copies
+
+    def gather_max(stage, copies):
+        for copy in copies:
+            copy.wait_recv()
+        return functools.reduce(
+            jnp.maximum, [tops_in[sent + d] for d in range(len(stages[stage]))], tops[stage]
+        )
+
+    top = jnp.max(jnp.max(wide[...], axis=1, keepdims=True), axis=0, keepdims=True)
+    tops[0] = jnp.broadcast_to(top, tops.shape[1:])
+    flying = send_max(0)
+    sends += flying
+
     def potential(x):
         return wide[pl.ds(x, 1), :]
 
@@ -207,12 +238,21 @@
         centre_plane = u[i + 1]
         v[i] = dot2(centre_plane, matrix[...]) + potential(i + lower) * centre_plane - 0.5 * (u[i] + u[i + 2])
 
-    for copy in m2_copies:
-        copy.wait_recv()
+    @pl.loop(0, length // 2)
+    def _(pair):
+        own_u[:, pair_lanes(pair)] = own_cells(u[2 * pair + 1], u[2 * pair + 2])
+        own_v[:, pair_lanes(pair)] = own_cells(v[2 * pair], v[2 * pair + 1])
+
+    for stage in range(1, len(stages)):
+        tops[stage] = gather_max(stage - 1, flying)
+        sent += len(stages[stage - 1])
+        flying = send_max(stage)
+        sends += flying
+    top = gather_max(len(stages) - 1, flying)
     for f in shared[2:]:
         v_copies[f].start()
 
-    top = functools.reduce(jnp.maximum, [max2[d] for d in range(sizes[1] * sizes[2])])[0:1, 0:1] + 6.0
+    top = top[0:1, 0:1] + 6.0
     centre = (top + CUTOFF) / 2.0
     width = (top - CUTOFF) / 2.0
     away = centre - SHIFT
@@ -220,15 +260,7 @@
     beta = -2.0 * away * alpha
     gamma = away * away * alpha - 1.0
 
-    def filtered(i):
-        return alpha * v[i] + beta * u[i + 1] + gamma * w(i + 2)
-
-    @pl.loop(0, length // 2)
-    def _(pair):
-        here = pl.ds(pl.multiple_of(pair * 2 * area, 2 * area), 2 * area)
-        rest[:, here] = dot2(filtered(2 * pair), select[0]) + dot2(filtered(2 * pair + 1), select[1])
-
-    r = rest[...]
+    r = alpha * own_v[...] + beta * own_u[...] + gamma * own_w[...]
     r_s = split(r)
     gram = dot3(r_s, r_s, NT)
     sigma = jnp.sqrt(jnp.sum(jnp.sum(gram * gram, axis=1, keepdims=True), axis=0, keepdims=True))
@@ -345,7 +377,8 @@
     cols = coefficients.shape[-1]
     doubled, area = 2 * length, length * length
     plane, lanes = doubled * doubled, length * doubled
-    others = sizes[1] * sizes[2]
+    stages = max_stages(sizes)
+    top_copies = max(sum(len(stage) for stage in stages), 1)
     dma = pltpu.SemaphoreType.DMA
     result = pl.pallas_call(
         functools.partial(kernel, length, sizes),
@@ -360,11 +393,13 @@
             pltpu.VMEM((length, length, length), F32),
             pltpu.VMEM((rows, cols), F32),
             pltpu.VMEM((8, length, lanes), F32),
-            pltpu.VMEM((sizes[0], 8, 128), F32),
-            pltpu.VMEM((others, 8, 128), F32),
+            pltpu.VMEM((len(stages), 8, 128), F32),
+            pltpu.VMEM((top_copies, 8, 128), F32),
             pltpu.VMEM((doubled, plane), F32),
             pltpu.VMEM((length + 2, rows, plane), F32),
             pltpu.VMEM((length, rows, plane), F32),
+            pltpu.VMEM((rows, length * area), F32),
+            pltpu.VMEM((rows, length * area), F32),
             pltpu.VMEM((rows, length * area), F32),
             pltpu.VMEM((6 * area, rows), F32),
             pltpu.VMEM((6 * area, rows), F32),
@@ -375,10 +410,8 @@
             dma((3,)),
             dma((7,)),
             dma((7,)),
-            dma((max(sizes[0] - 1, 1),)),
-            dma((max(sizes[0] - 1, 1),)),
-            dma((max(others - 1, 1),)),
-            dma((max(others - 1, 1),)),
+            dma((top_copies,)),
+            dma((top_copies,)),
             dma((6,)),
             dma((6,)),
             dma((6,)),

time: 34.6 us -> 33.9 us (0.980)
  Pallas kernels: 32.9 us -> 32.2 us
    pallas_call x1, Pallas kernels: 32.9 us -> 32.2 us  [per_device(): pl.pallas_call(functools.partial(kernel, length, sizes), out_shape=jax.Sh...]
where the time goes in v5:
time: 33.9 us; the launch traced here: 33.7 us
  Pallas kernels  32.2 us (95%)
  local copies, waits for them, and re-layouts  1.54 us (5%)
    pallas_call x1, Pallas kernels, per_device(): pl.pallas_call(functools.partial(kernel, length, sizes), out_shape=jax.Sh...  32.2 us
    unnamed x1, local copies, waits for them, and re-layouts  1.54 us

profile of v5, /device:TPU:0, one launch (start us, length us, event | category | flops | bytes accessed | tf_op | source)
XLA Modules:
  0.0 33.7 jit_solution(3287451333285421380)
XLA Ops:
  0.0 32.2 %shard_map.37 = f32[96,256]{1,0:T(8,128)} custom-call(f32[96,4096]{1,0:T(8,128)} %bitcast.3, f32[8,8,8]{2,1,0:T(8,128)} %pot_hbm.1, f32[96,256]{1,0:T(8,128)} %bitcast.5), custom_call_target="tpu_custom_call" | custom-call | tf_op jit(solution)/shard_map/pallas_call | solution.py:383
  32.2 1.5 %copy.5 = f32[1,1,1,96,256]{4,3,2,1,0:T(8,128)} copy(f32[1,1,1,96,256]{4,3,2,1,0:T(8,128)} %bitcast.4) | data formatting | bytes 196608

commit v6 on v5

--- a/solution.py
+++ b/solution.py
@@ -91,8 +91,13 @@
     plane, lower = doubled * doubled, length // 2
     half = cols // PARTS
 
+    moved = [[me[k]] + [lax.rem(me[k] + d, sizes[k]) for d in range(1, sizes[k])] for k in range(3)]
+
     def at(offset):
-        return tuple(lax.rem(me[k] + (offset[k] % sizes[k]), sizes[k]) for k in range(3))
+        return tuple(moved[k][offset[k] % sizes[k]] for k in range(3))
+
+    def finish(region, sem):
+        pltpu.make_async_copy(region, region, sem).wait()
 
     def remote(src, dst, send, recv, offset):
         return pltpu.make_async_remote_copy(
@@ -157,22 +162,17 @@
 
     pl.semaphore_wait(barrier, len(greeted))
 
-    sends = []
-    tile_copies = []
     for s, slot in enumerate(tile_slots):
-        copy = remote(tiles.at[own], tiles.at[s], tile_send.at[s], tile_recv.at[s], tile_to[slot])
+        copy = remote(tiles.at[own], tiles.at[s], tile_send, tile_recv, tile_to[slot])
         copy.start()
-        tile_copies.append(copy)
-    sends += tile_copies
 
     load_coef.wait()
     v_copies = {}
     shared = [f for f in range(6) if f % 2 == 0 or sizes[f // 2] > 2]
-    for f in shared:
-        v_copies[f] = remote(coef, v_in.at[f ^ 1], v_send.at[f], v_recv.at[f ^ 1], faces[f])
+    for k, f in enumerate(shared):
+        v_copies[f] = remote(coef, v_in.at[k], v_send, v_recv, faces[f])
     for f in shared[:2]:
         v_copies[f].start()
-    sends += v_copies.values()
 
     load_orb.wait()
 
@@ -193,38 +193,31 @@
     def _(pair):
         own_w[:, pair_lanes(pair)] = own_cells(w(2 * pair + 2), w(2 * pair + 3))
 
-    for copy in tile_copies:
-        copy.wait_recv()
+    finish(tiles.at[pl.ds(0, own)], tile_recv)
     for a in range(2):
         for b in range(2):
             low, high = tiles[4 * a + 2 * b], tiles[4 * a + 2 * b + 1]
             wide[pl.ds(a * length, length), pl.ds(b * lanes, lanes)] = low + pltpu.roll(high, length, 1)
 
     sent = 0
-    flying = []
 
     def send_max(stage):
-        copies = []
         for d, offset in enumerate(stages[stage]):
             k = sent + d
             copy = remote(
-                tops.at[stage], tops_in.at[k], top_send.at[k], top_recv.at[k], offset
+                tops.at[stage], tops_in.at[k], top_send.at[stage], top_recv.at[stage], offset
             )
             copy.start()
-            copies.append(copy)
-        return copies
-
-    def gather_max(stage, copies):
-        for copy in copies:
-            copy.wait_recv()
+
+    def gather_max(stage):
+        finish(tops_in.at[pl.ds(sent, len(stages[stage]))], top_recv.at[stage])
         return functools.reduce(
             jnp.maximum, [tops_in[sent + d] for d in range(len(stages[stage]))], tops[stage]
         )
 
     top = jnp.max(jnp.max(wide[...], axis=1, keepdims=True), axis=0, keepdims=True)
     tops[0] = jnp.broadcast_to(top, tops.shape[1:])
-    flying = send_max(0)
-    sends += flying
+    send_max(0)
 
     def potential(x):
         return wide[pl.ds(x, 1), :]
@@ -244,11 +237,10 @@
         own_v[:, pair_lanes(pair)] = own_cells(v[2 * pair], v[2 * pair + 1])
 
     for stage in range(1, len(stages)):
-        tops[stage] = gather_max(stage - 1, flying)
+        tops[stage] = gather_max(stage - 1)
         sent += len(stages[stage - 1])
-        flying = send_max(stage)
-        sends += flying
-    top = gather_max(len(stages) - 1, flying)
+        send_max(stage)
+    top = gather_max(len(stages) - 1)
     for f in shared[2:]:
         v_copies[f].start()
 
@@ -289,7 +281,6 @@
 
     rest_faces_s = split(rest_faces[...])
     facet[...] = dot3(rest_faces_s, root_s, NT)
-    f_copies = []
     face_copies = []
     for f, offset in enumerate(faces):
         if sizes[f // 2] > 2:
@@ -298,10 +289,8 @@
             both = pl.ds(f * area, 2 * area)
             face_copies.append((f, both, both, offset))
     for f, here, there, offset in face_copies:
-        copy = remote(facet.at[here, :], ft_in.at[there, :], f_send.at[f], f_recv.at[f], offset)
+        copy = remote(facet.at[here, :], ft_in.at[there, :], f_send, f_recv, offset)
         copy.start()
-        f_copies.append(copy)
-    sends += f_copies
 
     facet_s = split(facet[...])
     inverse_width = 1.0 / width
@@ -327,48 +316,49 @@
 
     prior = coef[...]
     current = dot3(diagonal, split(prior))
-    for copy in v_copies.values():
-        copy.wait_recv()
-    came = [split(v_in[f if f ^ 1 in shared else f ^ 1]) for f in range(6)]
+    finish(tiles.at[pl.ds(0, own)], tile_send)
+    for stage in range(len(stages)):
+        finish(tops_in.at[pl.ds(0, len(stages[stage]))], top_send.at[stage])
+    finish(v_in.at[pl.ds(0, len(shared))], v_send)
+    finish(v_in.at[pl.ds(0, len(shared))], v_recv)
+    came = [split(v_in[shared.index(f ^ 1 if f ^ 1 in shared else f)]) for f in range(6)]
     carried = []
-    for copy in f_copies:
-        copy.wait_recv()
+    finish(ft_in, f_recv)
     for f in range(6):
         carried.append(dot3(split(ft_in[pl.ds(f * area, area), :]), came[f]))
     current = current + dot3(couple, split(jnp.concatenate(carried, axis=0)))
 
     def send_projected(number, part, vectors):
         p_out[number, part] = dot3(facet_s, split(vectors))
-        copies = []
         for f, here, there, offset in face_copies:
             copy = remote(
                 p_out.at[number, part, here, :], p_in.at[number, part, there, :],
-                p_send.at[number, part, f], p_recv.at[number, part, f], offset,
+                p_send.at[number, part], p_recv.at[number, part], offset,
             )
             copy.start()
-            copies.append(copy)
-        return copies
 
     prior = [prior[:, k * half : (k + 1) * half] for k in range(PARTS)]
     current = [current[:, k * half : (k + 1) * half] for k in range(PARTS)]
-    flying = [send_projected(0, part, current[part]) for part in range(PARTS)]
+    for part in range(PARTS):
+        send_projected(0, part, current[part])
+    finish(facet, f_send)
     for number in range(2):
-        following, next_flying = [], []
+        following = []
         for part in range(PARTS):
             mine = 2.0 * dot3(diagonal, split(current[part])) - prior[part]
-            for copy in flying[part]:
-                copy.wait_recv()
-            sends += flying[part]
+            if number == 1:
+                finish(p_out.at[0, part], p_send.at[0, part])
+            finish(p_in.at[number, part], p_recv.at[number, part])
             mine = mine + 2.0 * dot3(couple, split(p_in[number, part]))
             following.append(mine)
             if number == 0:
-                next_flying.append(send_projected(1, part, mine))
+                send_projected(1, part, mine)
             else:
                 out_ref[:, pl.ds(part * half, half)] = mine
-        prior, current, flying = current, following, next_flying
-
-    for copy in sends:
-        copy.wait_send()
+        prior, current = current, following
+
+    for part in range(PARTS):
+        finish(p_out.at[1, part], p_send.at[1, part])
 
 
 def per_device(sizes, orbitals, potential, coefficients):
@@ -408,16 +398,16 @@
             pltpu.VMEM((2, PARTS, 6 * area, cols // PARTS), F32),
             pltpu.VMEM((2, PARTS, 6 * area, cols // PARTS), F32),
             dma((3,)),
-            dma((7,)),
-            dma((7,)),
-            dma((top_copies,)),
-            dma((top_copies,)),
-            dma((6,)),
-            dma((6,)),
-            dma((6,)),
-            dma((6,)),
-            dma((2, PARTS, 6)),
-            dma((2, PARTS, 6)),
+            dma,
+            dma,
+            dma((max(len(stages), 1),)),
+            dma((max(len(stages), 1),)),
+            dma,
+            dma,
+            dma,
+            dma,
+            dma((2, PARTS)),
+            dma((2, PARTS)),
         ],
         compiler_params=pltpu.CompilerParams(
             collective_id=0, has_side_effects=True, vmem_limit_bytes=60 * 1024 * 1024

time: 33.9 us -> 33.1 us (0.976)
  Pallas kernels: 32.2 us -> 31.4 us
    pallas_call x1, Pallas kernels: 32.2 us -> 31.4 us  [per_device(): pl.pallas_call(functools.partial(kernel, length, sizes), out_shape=jax.Sh...]
where the time goes in v6:
time: 33.1 us; the launch traced here: 32.9 us
  Pallas kernels  31.4 us (95%)
  local copies, waits for them, and re-layouts  1.54 us (5%)
    pallas_call x1, Pallas kernels, per_device(): pl.pallas_call(functools.partial(kernel, length, sizes), out_shape=jax.Sh...  31.4 us
    unnamed x1, local copies, waits for them, and re-layouts  1.54 us

profile of v6, /device:TPU:0, one launch (start us, length us, event | category | flops | bytes accessed | tf_op | source)
XLA Modules:
  0.0 32.9 jit_solution(5618316813826797606)
XLA Ops:
  0.0 31.4 %shard_map.37 = f32[96,256]{1,0:T(8,128)} custom-call(f32[96,4096]{1,0:T(8,128)} %bitcast.3, f32[8,8,8]{2,1,0:T(8,128)} %pot_hbm.1, f32[96,256]{1,0:T(8,128)} %bitcast.5), custom_call_target="tpu_custom_call" | custom-call | tf_op jit(solution)/shard_map/pallas_call | solution.py:373
  31.4 1.5 %copy.5 = f32[1,1,1,96,256]{4,3,2,1,0:T(8,128)} copy(f32[1,1,1,96,256]{4,3,2,1,0:T(8,128)} %bitcast.4) | data formatting | bytes 196608

commit v7 on v6

--- a/solution.py
+++ b/solution.py
@@ -58,13 +58,15 @@
     return jnp.where(condition, 1.0, 0.0).astype(dtype)
 
 
-def plane_matrix(width):
+def plane_matrix(width, first):
     cells = width * width
-    row, col = iota((cells, 1), 0), iota((1, cells), 1)
-    gap = row - col
-    inside = lax.div(row, width) == lax.div(col, width)
-    near = ((jnp.abs(gap) == 1) & inside) | (jnp.abs(gap) == width)
-    return (jnp.where(gap == 0, 3.0 - SHIFT, 0.0) - 0.5 * flag(near)).astype(BF16)
+
+    def coordinates(lane):
+        return lax.rem(lax.div(lane, width) + first, width), lax.rem(lane, width)
+
+    (row_y, row_z), (col_y, col_z) = coordinates(iota((cells, 1), 0)), coordinates(iota((1, cells), 1))
+    gap = jnp.abs(row_y - col_y) + jnp.abs(row_z - col_z)
+    return jnp.where(gap == 0, 3.0 - SHIFT, jnp.where(gap == 1, -0.5, 0.0)).astype(BF16)
 
 
 def max_stages(sizes):
@@ -81,7 +83,7 @@
 
 def kernel(
     length, sizes, orb_hbm, pot_hbm, coef_hbm, out_ref,
-    matrix, select, pick, orb, pot, coef, tiles, tops, tops_in, wide, u, v, own_w, own_u, own_v, rest_faces, facet, ft_in, v_in, p_out, p_in,
+    matrix, pick, orb, pot, coef, tiles, tops, tops_in, wide, u, v, rest_faces, facet, ft_in, v_in, p_out, p_in,
     load_sem, tile_send, tile_recv, top_send, top_recv,
     v_send, v_recv, f_send, f_recv, p_send, p_recv,
 ):
@@ -134,25 +136,22 @@
     load_orb.start()
     load_coef.start()
 
-    matrix[...] = plane_matrix(doubled)
-    source, target = iota((plane, 1), 0), iota((1, 2 * area), 1)
-    inner = lax.rem(target, area)
-    wanted = (lower + lax.div(inner, length)) * doubled + lower + lax.rem(inner, length)
-    for k in range(2):
-        select[k] = flag(source == jnp.where(lax.div(target, area) == k, wanted, -1), BF16)
-    cells = length * area
+    matrix[...] = plane_matrix(doubled, lower)
+    lanes = length * doubled
+    cells = length * lanes
     cell = iota((1, cells), 1)
+    inner = iota((area, 1), 0)
+    major, minor = lax.div(inner, length), lax.rem(inner, length)
     for f in range(6):
-        inner = iota((area, 1), 0)
-        major, minor = lax.div(inner, length), lax.rem(inner, length)
         layer = (length - 1) * (f % 2)
         picked_cell = (
-            layer * area + inner, major * area + layer * length + minor, major * area + minor * length + layer
+            layer * lanes + major * doubled + lower + minor,
+            major * lanes + layer * doubled + lower + minor,
+            major * lanes + minor * doubled + lower + layer,
         )[f // 2]
         pick[pl.ds(f * area, area), :] = flag(cell == picked_cell, BF16)
 
     load_pot.wait()
-    lanes = length * doubled
     flat = pot[...].reshape(area, length)
     spread = flag(lax.rem(iota((1, lanes), 1), doubled) == iota((length, 1), 0))
     keep = lax.div(iota((1, lanes), 1), doubled) == lax.rem(iota((area, 1), 0), length)
@@ -179,25 +178,23 @@
     def w(i):
         return orb[:, pl.ds(pl.multiple_of(i * plane, plane), plane)]
 
-    def pair_lanes(pair):
-        return pl.ds(pl.multiple_of(pair * 2 * area, 2 * area), 2 * area)
-
-    def own_cells(even, odd):
-        return dot2(even, select[0]) + dot2(odd, select[1])
-
-    @pl.loop(0, length + 2, unroll=2)
+    @pl.loop(0, length + 4, unroll=4)
+    def _(i):
+        here = pl.ds(pl.multiple_of(i * plane, plane), plane)
+        orb[:, here] = pltpu.roll(orb[:, here], plane - lower * doubled, 1)
+
+    @pl.loop(0, length + 2, unroll=5)
     def _(i):
         u[i] = dot2(w(i + 1), matrix[...]) - 0.5 * (w(i) + w(i + 2))
 
-    @pl.loop(0, length // 2)
-    def _(pair):
-        own_w[:, pair_lanes(pair)] = own_cells(w(2 * pair + 2), w(2 * pair + 3))
-
     finish(tiles.at[pl.ds(0, own)], tile_recv)
     for a in range(2):
+        quarters = []
         for b in range(2):
-            low, high = tiles[4 * a + 2 * b], tiles[4 * a + 2 * b + 1]
-            wide[pl.ds(a * length, length), pl.ds(b * lanes, lanes)] = low + pltpu.roll(high, length, 1)
+            quarters.append(tiles[4 * a + 2 * b] + pltpu.roll(tiles[4 * a + 2 * b + 1], length, 1))
+        wide[pl.ds(a * length, length), :] = pltpu.roll(
+            jnp.concatenate(quarters, axis=1), plane - lower * doubled, 1
+        )
 
     sent = 0
 
@@ -226,15 +223,15 @@
     def _(i):
         u[i] = u[i] + potential(i + lower - 1) * w(i + 1)
 
-    @pl.loop(0, length, unroll=2)
+    near = pl.ds(0, lanes)
+
+    @pl.loop(0, length, unroll=4)
     def _(i):
-        centre_plane = u[i + 1]
-        v[i] = dot2(centre_plane, matrix[...]) + potential(i + lower) * centre_plane - 0.5 * (u[i] + u[i + 2])
-
-    @pl.loop(0, length // 2)
-    def _(pair):
-        own_u[:, pair_lanes(pair)] = own_cells(u[2 * pair + 1], u[2 * pair + 2])
-        own_v[:, pair_lanes(pair)] = own_cells(v[2 * pair], v[2 * pair + 1])
+        v[i] = (
+            dot2(u[i + 1], matrix[:, near])
+            + potential(i + lower)[:, :lanes] * u[i + 1, :, near]
+            - 0.5 * (u[i, :, near] + u[i + 2, :, near])
+        )
 
     for stage in range(1, len(stages)):
         tops[stage] = gather_max(stage - 1)
@@ -252,7 +249,13 @@
     beta = -2.0 * away * alpha
     gamma = away * away * alpha - 1.0
 
-    r = alpha * own_v[...] + beta * own_u[...] + gamma * own_w[...]
+    z = lax.rem(iota((1, lanes), 1), doubled)
+    inside = flag((z >= lower) & (z < lower + length))
+    alpha, beta, gamma = alpha * inside, beta * inside, gamma * inside
+    planes = []
+    for i in range(length):
+        planes.append(alpha * v[i] + beta * u[i + 1, :, near] + gamma * orb[:, pl.ds((i + 2) * plane, lanes)])
+    r = jnp.concatenate(planes, axis=1)
     r_s = split(r)
     gram = dot3(r_s, r_s, NT)
     sigma = jnp.sqrt(jnp.sum(jnp.sum(gram * gram, axis=1, keepdims=True), axis=0, keepdims=True))
@@ -299,13 +302,9 @@
         slots.append(rest_faces[pl.ds((f if sizes[f // 2] > 2 else f ^ 1) * area, area), :])
     slots_s = split(jnp.concatenate(slots, axis=0))
     couple = split((-0.5 * inverse_width) * dot3(root_s, slots_s, NT))
-    own_wide = dot2(wide[pl.ds(lower, length), :], select[0])
-    own_odd = pltpu.roll(own_wide, area, 1)
-    own_potential = jnp.concatenate(
-        [own_wide[k : k + 1, :] + own_odd[k + 1 : k + 2, :] for k in range(0, length, 2)], axis=1
-    )
-    around = jnp.zeros_like(r)
-    for stride in (area, length, 1):
+    own_potential = jnp.concatenate([wide[pl.ds(lower + k, 1), near] for k in range(length)], axis=1)
+    around = pltpu.roll(r, 1, 1) + pltpu.roll(r, cells - 1, 1)
+    for stride in (lanes, doubled):
         coordinate = lax.rem(lax.div(cell, stride), length)
         around = around + flag(coordinate > 0) * pltpu.roll(r, stride, 1)
         around = around + flag(coordinate < length - 1) * pltpu.roll(r, cells - stride, 1)
@@ -377,8 +376,7 @@
         out_specs=pl.BlockSpec(memory_space=pltpu.VMEM),
         scratch_shapes=[
             pltpu.VMEM((plane, plane), BF16),
-            pltpu.VMEM((2, plane, 2 * area), BF16),
-            pltpu.VMEM((6 * area, length * area), BF16),
+            pltpu.VMEM((6 * area, length * lanes), BF16),
             pltpu.VMEM((rows, (length + 4) * plane), F32),
             pltpu.VMEM((length, length, length), F32),
             pltpu.VMEM((rows, cols), F32),
@@ -387,10 +385,7 @@
             pltpu.VMEM((top_copies, 8, 128), F32),
             pltpu.VMEM((doubled, plane), F32),
             pltpu.VMEM((length + 2, rows, plane), F32),
-            pltpu.VMEM((length, rows, plane), F32),
-            pltpu.VMEM((rows, length * area), F32),
-            pltpu.VMEM((rows, length * area), F32),
-            pltpu.VMEM((rows, length * area), F32),
+            pltpu.VMEM((length, rows, lanes), F32),
             pltpu.VMEM((6 * area, rows), F32),
             pltpu.VMEM((6 * area, rows), F32),
             pltpu.VMEM((6 * area, rows), F32),

time: 33.1 us -> 33.5 us (1.012)
  Pallas kernels: 31.4 us -> 31.8 us
    pallas_call x1, Pallas kernels: 31.4 us -> 31.8 us  [per_device(): pl.pallas_call(functools.partial(kernel, length, sizes), out_shape=jax.Sh...]
where the time goes in v7:
time: 33.5 us; the launch traced here: 33.3 us
  Pallas kernels  31.8 us (95%)
  local copies, waits for them, and re-layouts  1.54 us (5%)
    pallas_call x1, Pallas kernels, per_device(): pl.pallas_call(functools.partial(kernel, length, sizes), out_shape=jax.Sh...  31.8 us
    unnamed x1, local copies, waits for them, and re-layouts  1.54 us

profile of v7, /device:TPU:0, one launch (start us, length us, event | category | flops | bytes accessed | tf_op | source)
XLA Modules:
  0.0 33.3 jit_solution(5367534206024375460)
XLA Ops:
  0.0 31.8 %shard_map.37 = f32[96,256]{1,0:T(8,128)} custom-call(f32[96,4096]{1,0:T(8,128)} %bitcast.3, f32[8,8,8]{2,1,0:T(8,128)} %pot_hbm.1, f32[96,256]{1,0:T(8,128)} %bitcast.5), custom_call_target="tpu_custom_call" | custom-call | tf_op jit(solution)/shard_map/pallas_call | solution.py:372
  31.8 1.5 %copy.5 = f32[1,1,1,96,256]{4,3,2,1,0:T(8,128)} copy(f32[1,1,1,96,256]{4,3,2,1,0:T(8,128)} %bitcast.4) | data formatting | bytes 196608

commit v8 on v6

--- a/solution.py
+++ b/solution.py
@@ -185,11 +185,11 @@
     def own_cells(even, odd):
         return dot2(even, select[0]) + dot2(odd, select[1])
 
-    @pl.loop(0, length + 2, unroll=2)
+    @pl.loop(0, length + 2, unroll=5)
     def _(i):
         u[i] = dot2(w(i + 1), matrix[...]) - 0.5 * (w(i) + w(i + 2))
 
-    @pl.loop(0, length // 2)
+    @pl.loop(0, length // 2, unroll=2)
     def _(pair):
         own_w[:, pair_lanes(pair)] = own_cells(w(2 * pair + 2), w(2 * pair + 3))
 
@@ -226,12 +226,12 @@
     def _(i):
         u[i] = u[i] + potential(i + lower - 1) * w(i + 1)
 
-    @pl.loop(0, length, unroll=2)
+    @pl.loop(0, length, unroll=4)
     def _(i):
         centre_plane = u[i + 1]
         v[i] = dot2(centre_plane, matrix[...]) + potential(i + lower) * centre_plane - 0.5 * (u[i] + u[i + 2])
 
-    @pl.loop(0, length // 2)
+    @pl.loop(0, length // 2, unroll=2)
     def _(pair):
         own_u[:, pair_lanes(pair)] = own_cells(u[2 * pair + 1], u[2 * pair + 2])
         own_v[:, pair_lanes(pair)] = own_cells(v[2 * pair], v[2 * pair + 1])
@@ -255,13 +255,10 @@
     r = alpha * own_v[...] + beta * own_u[...] + gamma * own_w[...]
     r_s = split(r)
     gram = dot3(r_s, r_s, NT)
+    rest_faces[...] = dot(pick[...], r_s[0], NT) + dot(pick[...], r_s[1], NT)
     sigma = jnp.sqrt(jnp.sum(jnp.sum(gram * gram, axis=1, keepdims=True), axis=0, keepdims=True))
     eye = flag(iota((rows, rows), 0) == iota((rows, rows), 1))
     product = gram * (1.0 / sigma)
-
-    def pick_face(f):
-        here = pl.ds(pl.multiple_of(f * area, area), area)
-        rest_faces[here, :] = dot(pick[here, :], r_s[0], NT) + dot(pick[here, :], r_s[1], NT)
 
     def newton(step, state):
         product, inverse = state
@@ -269,12 +266,9 @@
         factor_s = split(factor)
         once = dot3(split(product), factor_s)
         inverse = dot3(split(inverse), factor_s)
-        pick_face(step)
         return dot3(split(once), factor_s), inverse
 
     product, inverse = lax.fori_loop(0, NEWTON - 1, newton, (product, eye))
-    for f in range(NEWTON - 1, 6):
-        pick_face(f)
     inverse = dot3(split(inverse), split(1.5 * eye - 0.5 * product))
     root = inverse * lax.rsqrt(sigma)
     root_s = split(root)

time: 33.1 us -> 33 us (level)
  no operation moved by 1% of the time
where the time goes in v8:
time: 33 us; the launch traced here: 32.9 us
  Pallas kernels  31.3 us (95%)
  local copies, waits for them, and re-layouts  1.54 us (5%)
    pallas_call x1, Pallas kernels, per_device(): pl.pallas_call(functools.partial(kernel, length, sizes), out_shape=jax.Sh...  31.3 us
    unnamed x1, local copies, waits for them, and re-layouts  1.54 us

profile of v8, /device:TPU:0, one launch (start us, length us, event | category | flops | bytes accessed | tf_op | source)
XLA Modules:
  0.0 32.9 jit_solution(9400656783128746795)
XLA Ops:
  0.0 31.3 %shard_map.37 = f32[96,256]{1,0:T(8,128)} custom-call(f32[96,4096]{1,0:T(8,128)} %bitcast.3, f32[8,8,8]{2,1,0:T(8,128)} %pot_hbm.1, f32[96,256]{1,0:T(8,128)} %bitcast.5), custom_call_target="tpu_custom_call" | custom-call | tf_op jit(solution)/shard_map/pallas_call | solution.py:367
  31.4 1.5 %copy.5 = f32[1,1,1,96,256]{4,3,2,1,0:T(8,128)} copy(f32[1,1,1,96,256]{4,3,2,1,0:T(8,128)} %bitcast.4) | data formatting | bytes 196608

commit v9 on v8

--- a/solution.py
+++ b/solution.py
@@ -171,8 +171,6 @@
     shared = [f for f in range(6) if f % 2 == 0 or sizes[f // 2] > 2]
     for k, f in enumerate(shared):
         v_copies[f] = remote(coef, v_in.at[k], v_send, v_recv, faces[f])
-    for f in shared[:2]:
-        v_copies[f].start()
 
     load_orb.wait()
 
@@ -241,7 +239,7 @@
         sent += len(stages[stage - 1])
         send_max(stage)
     top = gather_max(len(stages) - 1)
-    for f in shared[2:]:
+    for f in shared:
         v_copies[f].start()
 
     top = top[0:1, 0:1] + 6.0

time: 33 us -> 33.4 us (1.012)
  Pallas kernels: 31.3 us -> 31.7 us
    pallas_call x1, Pallas kernels: 31.3 us -> 31.7 us  [per_device(): pl.pallas_call(functools.partial(kernel, length, sizes), out_shape=jax.Sh...]
where the time goes in v9:
time: 33.4 us; the launch traced here: 33.2 us
  Pallas kernels  31.7 us (95%)
  local copies, waits for them, and re-layouts  1.54 us (5%)
    pallas_call x1, Pallas kernels, per_device(): pl.pallas_call(functools.partial(kernel, length, sizes), out_shape=jax.Sh...  31.7 us
    unnamed x1, local copies, waits for them, and re-layouts  1.54 us

profile of v9, /device:TPU:0, one launch (start us, length us, event | category | flops | bytes accessed | tf_op | source)
XLA Modules:
  0.0 33.2 jit_solution(6138523657152084083)
XLA Ops:
  0.0 31.7 %shard_map.37 = f32[96,256]{1,0:T(8,128)} custom-call(f32[96,4096]{1,0:T(8,128)} %bitcast.3, f32[8,8,8]{2,1,0:T(8,128)} %pot_hbm.1, f32[96,256]{1,0:T(8,128)} %bitcast.5), custom_call_target="tpu_custom_call" | custom-call | tf_op jit(solution)/shard_map/pallas_call | solution.py:365
  31.7 1.5 %copy.5 = f32[1,1,1,96,256]{4,3,2,1,0:T(8,128)} copy(f32[1,1,1,96,256]{4,3,2,1,0:T(8,128)} %bitcast.4) | data formatting | bytes 196608

commit v10 on v8

--- a/solution.py
+++ b/solution.py
@@ -189,10 +189,6 @@
     def _(i):
         u[i] = dot2(w(i + 1), matrix[...]) - 0.5 * (w(i) + w(i + 2))
 
-    @pl.loop(0, length // 2, unroll=2)
-    def _(pair):
-        own_w[:, pair_lanes(pair)] = own_cells(w(2 * pair + 2), w(2 * pair + 3))
-
     finish(tiles.at[pl.ds(0, own)], tile_recv)
     for a in range(2):
         for b in range(2):
@@ -233,6 +229,7 @@
 
     @pl.loop(0, length // 2, unroll=2)
     def _(pair):
+        own_w[:, pair_lanes(pair)] = own_cells(w(2 * pair + 2), w(2 * pair + 3))
         own_u[:, pair_lanes(pair)] = own_cells(u[2 * pair + 1], u[2 * pair + 2])
         own_v[:, pair_lanes(pair)] = own_cells(v[2 * pair], v[2 * pair + 1])
 

time: 33 us -> 33 us (level)
  no operation moved by 1% of the time
where the time goes in v10:
time: 33 us; the launch traced here: 32.9 us
  Pallas kernels  31.3 us (95%)
  local copies, waits for them, and re-layouts  1.54 us (5%)
    pallas_call x1, Pallas kernels, per_device(): pl.pallas_call(functools.partial(kernel, length, sizes), out_shape=jax.Sh...  31.3 us
    unnamed x1, local copies, waits for them, and re-layouts  1.54 us

profile of v10, /device:TPU:0, one launch (start us, length us, event | category | flops | bytes accessed | tf_op | source)
XLA Modules:
  0.0 32.9 jit_solution(11912209476729868820)
XLA Ops:
  0.0 31.3 %shard_map.37 = f32[96,256]{1,0:T(8,128)} custom-call(f32[96,4096]{1,0:T(8,128)} %bitcast.3, f32[8,8,8]{2,1,0:T(8,128)} %pot_hbm.1, f32[96,256]{1,0:T(8,128)} %bitcast.5), custom_call_target="tpu_custom_call" | custom-call | tf_op jit(solution)/shard_map/pallas_call | solution.py:364
  31.4 1.5 %copy.5 = f32[1,1,1,96,256]{4,3,2,1,0:T(8,128)} copy(f32[1,1,1,96,256]{4,3,2,1,0:T(8,128)} %bitcast.4) | data formatting | bytes 196608
